TPU v7x, 32 devices: a whole 2x2x4 slice. The times are simulated.
32 devices in a mesh: head: 4 (over x, core), seq: 8 (over z, y).
Axes of the slice: x: 2, y: 2, z: 4, core: 2. Of those that a mesh axis runs over, the one named last changes fastest.
Arguments:
- tokens: bfloat16 [4096, 4, 768], P('seq'), may hold values from -6 to 6
- attn_gain: float32 [768], replicated, may hold values from 0.5 to 1.5
- qkv_weight: bfloat16 [768, 2304], P(None, 'head'), may hold values from -0.21875 to 0.21875
- bias_table: float32 [32, 12], P(None, 'head'), may hold values from -4 to 4
- proj_weight: bfloat16 [768, 768], P('head'), may hold values from -6 to 6
- ffn_gain: float32 [768], replicated, may hold values from 0.5 to 1.5
- router_weight: bfloat16 [768, 32], replicated, may hold values from -0.15625 to 0.15625
- router_bias: float32 [32], replicated, may hold values from -3 to 3
- expert_in: bfloat16 [32, 768, 3072], P(('head', 'seq')), may hold values from -0.21875 to 0.21875
- expert_out: bfloat16 [32, 3072, 768], P(('head', 'seq')), may hold values from -6 to 6
- bucket: int32 [8192], replicated, may hold values from 0 to 31
- expert_choice: int32 [4096, 4], P('seq', 'head'), may hold values from 0 to 31
- priority: int32 [4096, 4], P('seq', 'head'), may hold values from 0 to 16383, as said below
- out_grad: bfloat16 [4096, 4, 768], P('seq', 'head'), may hold values from -6 to 6
Outputs:
- output: bfloat16 [4096, 4, 768], P('seq', 'head')
- grad_tokens: bfloat16 [4096, 4, 768], P('seq', 'head')
- grad_attn_gain: float32 [768], replicated
- grad_qkv_weight: float32 [768, 2304], P(None, 'head')
- grad_bias_table: float32 [32, 12], P(None, 'head')
- grad_proj_weight: float32 [768, 768], P('head')
- grad_ffn_gain: float32 [768], replicated
- grad_router_weight: float32 [768, 32], replicated
- grad_router_bias: float32 [32], replicated
- grad_expert_in: float32 [32, 768, 3072], P(('head', 'seq'))
- grad_expert_out: float32 [32, 3072, 768], P(('head', 'seq'))
Inputs may be any that keep to these rules, and one draw needn't show every extreme that they name: `priority`: each number occurs once.
All inputs are finite; a program needn't handle non-finite values.
Results may differ from a plain program's by a relative error of at most 0.019.
Values may be sent and summed in bfloat16 or wider, within the bound.
A program may use at most 1.3125 GiB of HBM per device.

v0:
```python
import math

import jax
import jax.numpy as jnp
from jax import lax
from jax.sharding import PartitionSpec as P

eps = 1e-06
scaling = 0.125
HIGH = lax.Precision.HIGHEST


def rms_forward(values, gain):
    inverse = lax.rsqrt(jnp.mean(values * values, axis=-1, keepdims=True) + eps)
    return (values * inverse * gain, inverse)


def rms_backward(values, inverse, gain, upstream):
    normed = values * inverse
    scaled = upstream * gain
    inner = jnp.mean(scaled * normed, axis=-1, keepdims=True)
    return (inverse * (scaled - normed * inner), jnp.sum(upstream * normed, axis=(0, 1)))


def split_groups(values, groups):
    shaped = values.reshape((values.shape[0], groups, values.shape[1] // groups) + values.shape[2:])
    return jnp.moveaxis(shaped, 1, 0)


def join_groups(values):
    moved = jnp.moveaxis(values, 0, 1)
    return moved.reshape((moved.shape[0], moved.shape[1] * moved.shape[2]) + moved.shape[3:])


def block_scores(query, keys, rel_taken):
    raw = jnp.einsum("ibhd,jbhd->bhij", query, keys, preferred_element_type=jnp.float32)
    return raw * scaling + rel_taken[None]


def toeplitz(rel_bias, corner, rows, cols):
    count = rows + cols
    heads = rel_bias.shape[0]
    window = lax.dynamic_slice_in_dim(rel_bias, corner - rows, count, 1)
    wheel = jnp.concatenate([window[:, rows:], window[:, :rows]], axis=1)
    tiled = jnp.broadcast_to(wheel[:, None, :], (heads, rows, count)).reshape(heads, rows * count)
    return tiled[:, : rows * (count - 1)].reshape(heads, rows, count - 1)[:, :, :cols]


def toeplitz_back(grad, corner, rows, cols, total):
    count = rows + cols
    heads = grad.shape[0]
    padded = jnp.pad(grad, ((0, 0), (0, 0), (0, count - 1 - cols))).reshape(
        heads, rows * (count - 1)
    )
    padded = jnp.pad(padded, ((0, 0), (0, rows))).reshape(heads, rows, count)
    wheel = jnp.sum(padded, axis=1)
    window = jnp.concatenate([wheel[:, cols:], wheel[:, :cols]], axis=1)
    return lax.dynamic_update_slice_in_dim(
        jnp.zeros((heads, total), jnp.float32), window, corner - rows, 1
    )


def local(
    tokens,
    attn_gain,
    qkv_weight,
    bias_table,
    proj_weight,
    ffn_gain,
    router_weight,
    router_bias,
    expert_in,
    expert_out,
    bucket,
    expert_choice,
    priority,
    out_grad,
):
    f32 = jnp.float32
    bf16 = jnp.bfloat16
    tsd, seqs, width = tokens.shape
    heads_here = bias_table.shape[1]
    head_dim = qkv_weight.shape[1] // (3 * heads_here)
    hidden_width = heads_here * head_dim
    length = bucket.shape[0] // 2
    own = out_grad.shape[1]
    group = math.gcd(seqs, max(1, 512 // tsd))
    groups = seqs // group
    seq_index = lax.axis_index("seq")
    head_index = lax.axis_index("head")
    xf = tokens.astype(f32)
    normed1_f, inv1 = rms_forward(xf, attn_gain)
    normed1 = normed1_f.astype(bf16).reshape(tsd * seqs, width)
    qkv = jnp.dot(normed1, qkv_weight, preferred_element_type=f32).astype(bf16)
    qkv = qkv.reshape(tsd, seqs, heads_here, 3, head_dim)
    query, keys, vals = (qkv[:, :, :, 0], qkv[:, :, :, 1], qkv[:, :, :, 2])
    all_keys, all_vals = (
        lax.all_gather(keys, "seq", axis=0, tiled=True),
        lax.all_gather(vals, "seq", axis=0, tiled=True),
    )
    onehot = (bucket[:, None] == jnp.arange(bias_table.shape[0], dtype=jnp.int32)[None, :]).astype(
        f32
    )
    rel_bias = jnp.einsum("om,mh->ho", onehot, bias_table, precision=HIGH)
    own_corner = length - seq_index * tsd
    rel_taken = toeplitz(rel_bias, own_corner, tsd, length)

    def attend_block(item):
        query_block, key_block, value_block = item
        scores = block_scores(query_block, key_block, rel_taken)
        top = jnp.max(scores, axis=3, keepdims=True)
        lse_block = top + jnp.log(jnp.sum(jnp.exp(scores - top), axis=3, keepdims=True))
        probs_block = jnp.exp(scores - lse_block).astype(bf16)
        out_block = jnp.einsum(
            "bhij,jbhd->ibhd", probs_block, value_block, preferred_element_type=f32
        ).astype(bf16)
        return (out_block, lse_block, probs_block)

    group_query = split_groups(query, groups)
    group_keys = split_groups(all_keys, groups)
    group_vals = split_groups(all_vals, groups)
    attended_g, lse_g, probs_g = lax.map(attend_block, (group_query, group_keys, group_vals))
    attended = join_groups(attended_g)
    probs_low = probs_g.reshape((seqs,) + probs_g.shape[2:])
    flat_attended = attended.reshape(tsd * seqs, hidden_width)
    partial_value = jnp.dot(flat_attended, proj_weight, preferred_element_type=f32).reshape(
        tsd, seqs, width
    )
    branch = lax.psum_scatter(partial_value, "head", scatter_dimension=1, tiled=True)
    x_own = lax.dynamic_slice_in_dim(xf, head_index * own, own, 1)
    inv1_own = lax.dynamic_slice_in_dim(inv1, head_index * own, own, 1)
    mid = x_own + branch
    normed2_f, inv2 = rms_forward(mid, ffn_gain)
    rows = tsd * own
    normed2 = normed2_f.astype(bf16).reshape(rows, width)
    experts = router_weight.shape[1]
    logits = jnp.dot(normed2, router_weight, preferred_element_type=f32) + router_bias
    gates = jax.nn.softmax(logits, axis=1)
    route = expert_choice.reshape(rows)
    order = priority.reshape(rows)
    same = (route[:, None] == route[None, :]) & (order[None, :] < order[:, None])
    rank = jnp.sum(same.astype(jnp.int32), axis=1)
    capacity = max(2, (5 * rows + 4 * experts - 1) // (4 * experts))
    keep = rank < capacity
    slot = route * capacity + jnp.minimum(rank, capacity - 1)
    placing = (
        (slot[None, :] == jnp.arange(experts * capacity, dtype=jnp.int32)[:, None]) & keep[None, :]
    ).astype(bf16)
    sending = (
        jnp.dot(placing, normed2, preferred_element_type=f32)
        .astype(bf16)
        .reshape(experts, capacity, width)
    )
    arriving = lax.all_to_all(sending, ("head", "seq"), split_axis=0, concat_axis=0, tiled=True)
    flat = arriving.reshape(-1, width)
    pre = jnp.dot(flat, expert_in[0], preferred_element_type=f32)
    act = jax.nn.gelu(pre, approximate=True).astype(bf16)
    result = jnp.dot(act, expert_out[0], preferred_element_type=f32).astype(bf16)
    returned = result.reshape(arriving.shape)
    pre_act = pre.reshape(arriving.shape[:2] + (pre.shape[1],))
    back = lax.all_to_all(returned, ("head", "seq"), split_axis=0, concat_axis=0, tiled=True)
    expert_rows = jnp.einsum(
        "sr,sd->rd", placing, back.reshape(experts * capacity, width), preferred_element_type=f32
    )
    chosen = (route[:, None] == jnp.arange(experts, dtype=jnp.int32)[None, :]).astype(f32)
    gate = jnp.sum(gates * chosen, axis=1)
    mixed = mid.reshape(rows, width) + gate[:, None] * expert_rows
    output = mixed.reshape(tsd, own, width).astype(bf16)
    upstream = out_grad.astype(f32).reshape(rows, width)
    grad_gate = jnp.sum(upstream * expert_rows, axis=1)
    grad_rows = (gate[:, None] * upstream).astype(bf16)
    to_send = (
        jnp.dot(placing, grad_rows, preferred_element_type=f32)
        .astype(bf16)
        .reshape(experts, capacity, width)
    )
    arriving_grad = lax.all_to_all(
        to_send, ("head", "seq"), split_axis=0, concat_axis=0, tiled=True
    )
    flat_grad = arriving_grad.reshape(-1, width)
    flat_pre = pre_act.reshape(-1, pre_act.shape[2])
    act_value, act_pull = jax.vjp(lambda v: jax.nn.gelu(v, approximate=True), flat_pre)
    act_low = act_value.astype(bf16)
    grad_act = jnp.einsum("sd,fd->sf", flat_grad, expert_out[0], preferred_element_type=f32)
    grad_pre = act_pull(grad_act)[0].astype(bf16)
    grad_expert_out = jnp.einsum("sf,sd->fd", act_low, flat_grad, preferred_element_type=f32)[None]
    grad_expert_in = jnp.einsum(
        "sd,sf->df", arriving.reshape(-1, width), grad_pre, preferred_element_type=f32
    )[None]
    grad_slots = jnp.einsum("sf,df->sd", grad_pre, expert_in[0], preferred_element_type=f32).astype(
        bf16
    )
    grad_back = lax.all_to_all(
        grad_slots.reshape(arriving_grad.shape),
        ("head", "seq"),
        split_axis=0,
        concat_axis=0,
        tiled=True,
    )
    grad_disp = jnp.einsum(
        "sr,sd->rd",
        placing,
        grad_back.reshape(experts * capacity, width),
        preferred_element_type=f32,
    )
    grad_logits = gates * (chosen - gate[:, None]) * grad_gate[:, None]
    grad_router_bias = jnp.sum(grad_logits, axis=0)
    grad_router_weight = jnp.einsum("rd,re->de", normed2.astype(f32), grad_logits, precision=HIGH)
    grad_normed2 = grad_disp + jnp.einsum(
        "re,de->rd", grad_logits, router_weight.astype(f32), precision=HIGH
    )
    grad_mid_norm, grad_ffn_gain = rms_backward(
        mid, inv2, ffn_gain, grad_normed2.reshape(tsd, own, width)
    )
    grad_mid = upstream.reshape(tsd, own, width) + grad_mid_norm
    grad_branch = lax.all_gather(grad_mid.astype(bf16), "head", axis=1, tiled=True)
    flat_branch = grad_branch.reshape(tsd * seqs, width)
    grad_proj_weight = jnp.einsum(
        "rc,rd->cd", flat_attended, flat_branch, preferred_element_type=f32
    )
    grad_attended = jnp.einsum(
        "rd,cd->rc", flat_branch, proj_weight, preferred_element_type=f32
    ).astype(bf16)
    grad_attended = grad_attended.reshape(tsd, seqs, heads_here, head_dim)

    def attend_back(item):
        query_block, key_block, value_block, grad_block, lse_block = item
        scores = block_scores(query_block, key_block, rel_taken)
        probs_block = jnp.exp(scores - lse_block)
        grad_probs = jnp.einsum(
            "ibhd,jbhd->bhij", grad_block, value_block, preferred_element_type=f32
        )
        delta_block = jnp.sum(probs_block * grad_probs, axis=3, keepdims=True)
        grad_block_scores = (probs_block * (grad_probs - delta_block)).astype(bf16)
        grad_block_query = (
            scaling
            * jnp.einsum(
                "bhij,jbhd->ibhd", grad_block_scores, key_block, preferred_element_type=f32
            )
        ).astype(bf16)
        return (grad_block_scores, grad_block_query, delta_block)

    group_grad = split_groups(grad_attended, groups)
    scores_g, grad_query_g, delta_g = lax.map(
        attend_back, (group_query, group_keys, group_vals, group_grad, lse_g)
    )
    grad_scores = scores_g.reshape((seqs,) + scores_g.shape[2:])
    grad_query = join_groups(grad_query_g)
    summed = jnp.sum(grad_scores, axis=0, dtype=f32)
    per_offset = toeplitz_back(summed, own_corner, tsd, length, 2 * length)
    grad_bias_table = jnp.einsum("om,ho->mh", onehot, per_offset, precision=HIGH)
    count = tsd * lax.axis_size("seq")
    grad_k = scaling * jnp.einsum("bhij,ibhd->jbhd", grad_scores, query, preferred_element_type=f32)
    grad_v = jnp.einsum("bhij,ibhd->jbhd", probs_low, grad_attended, preferred_element_type=f32)
    kv_summed = lax.psum_scatter(
        jnp.concatenate(
            [grad_k.reshape(count, seqs, hidden_width), grad_v.reshape(count, seqs, hidden_width)],
            axis=2,
        ).astype(jnp.bfloat16),
        "seq",
        scatter_dimension=0,
        tiled=True,
    ).astype(jnp.float32)
    grad_keys = kv_summed[:, :, :hidden_width]
    grad_vals = kv_summed[:, :, hidden_width:]
    grad_qkv = jnp.stack(
        [
            grad_query,
            grad_keys.astype(bf16).reshape(tsd, seqs, heads_here, head_dim),
            grad_vals.astype(bf16).reshape(tsd, seqs, heads_here, head_dim),
        ],
        axis=3,
    )
    grad_qkv = grad_qkv.reshape(tsd * seqs, 3 * hidden_width)
    grad_qkv_weight = jnp.einsum("rd,rc->dc", normed1, grad_qkv, preferred_element_type=f32)
    grad_normed1 = jnp.einsum(
        "rc,dc->rd", grad_qkv, qkv_weight, preferred_element_type=f32
    ).reshape(tsd, seqs, width)
    grad_normed1_own = lax.psum_scatter(
        grad_normed1.astype(jnp.bfloat16), "head", scatter_dimension=1, tiled=True
    ).astype(jnp.float32)
    grad_x_norm, grad_attn_gain = rms_backward(x_own, inv1_own, attn_gain, grad_normed1_own)
    grad_tokens = (grad_mid + grad_x_norm).astype(bf16)
    grad_qkv_weight, grad_proj_weight, grad_bias_table = (
        lax.psum(grad_qkv_weight.astype(jnp.bfloat16), "seq").astype(jnp.float32),
        lax.psum(grad_proj_weight.astype(jnp.bfloat16), "seq").astype(jnp.float32),
        lax.psum(grad_bias_table.astype(jnp.bfloat16), "seq").astype(jnp.float32),
    )
    grad_attn_gain, grad_ffn_gain, grad_router_weight, grad_router_bias = lax.psum(
        (grad_attn_gain, grad_ffn_gain, grad_router_weight, grad_router_bias), ("head", "seq")
    )
    return (
        output,
        grad_tokens,
        grad_attn_gain,
        grad_qkv_weight,
        grad_bias_table,
        grad_proj_weight,
        grad_ffn_gain,
        grad_router_weight,
        grad_router_bias,
        grad_expert_in,
        grad_expert_out,
    )


def solution(mesh):
    placed = (
        P("seq", None, None),
        P(),
        P(None, "head"),
        P(None, "head"),
        P("head", None),
        P(),
        P(),
        P(),
        P(("head", "seq"), None, None),
        P(("head", "seq"), None, None),
        P(),
        P("seq", "head"),
        P("seq", "head"),
        P("seq", "head", None),
    )
    return jax.shard_map(
        local,
        mesh=mesh,
        in_specs=placed,
        out_specs=(
            P("seq", "head", None),
            P("seq", "head", None),
            P(),
            P(None, "head"),
            P(None, "head"),
            P("head", None),
            P(),
            P(),
            P(),
            P(("head", "seq"), None, None),
            P(("head", "seq"), None, None),
        ),
        check_vma=False,
    )
```

profile of v0, /device:TPU:12, one launch (start us, length us, event | category | flops | bytes accessed | tf_op | source)
XLA Modules:
  0.0 2632.9 jit_solution(10814764440025706364)
XLA Ops:
  81.3 37.5 %copy.101 = f32[1,3,512,4608]{3,1,2,0:T(4,128)} copy(f32[1,3,512,4608]{3,2,1,0:T(8,128)} %broadcast_bitcast_fusion) | data formatting | bytes 56623104
  118.8 25.8 slice_bitcast_fusion
  151.2 524.9 %while.30 = (u32[]{:T(128)}, f32[1,3,2358784]{2,1,0:T(4,128)}, f32[7076352]{0:T(1024)}, u32[]{}, f32[]{:T(128)}, /*index=5*/u32[]{}, u32[]{}, u32[]{}) while((u32[]{:T(128)}, f32[1,3,2358784]{2,1,0:T(4,128)}, f32[7076352]{0:T(1024)}, u32[]{}, f32[]{:T(128)}, /*index=5*/u32[]{}, u32[]{}, u32[]{}) %tuple.86), condition=%wide.cond, body=%wide.body.sunk | while | flops 9 | bytes 37740744
  151.7 94.0 %dynamic-slice_reduce_fusion.2 = f32[2358784]{0:T(1024)} fusion(f32[]{:T(128)} %broadcast.171, f32[1,3,2358784]{2,1,0:T(4,128)} %get-tuple-element.453, u32[]{:T(128)S(6)} %multiply.47, u32[]{:T(128)S(6)} %multiply.48), kind=kLoop, calls=%fused_computation.169.clone.1 | loop fusion | bytes 18870284
  245.8 80.6 %dynamic-update-slice.4 = f32[7076352]{0:T(1024)} dynamic-update-slice(f32[7076352]{0:T(1024)} %get-tuple-element.446, f32[2358784]{0:T(1024)} %dynamic-slice_reduce_fusion.2, u32[]{:T(128)S(6)} %add.205) | dynamic-update-slice | bytes 18870276
  326.9 94.0 %dynamic-slice_reduce_fusion.2 = f32[2358784]{0:T(1024)} fusion(f32[]{:T(128)} %broadcast.171, f32[1,3,2358784]{2,1,0:T(4,128)} %get-tuple-element.453, u32[]{:T(128)S(6)} %multiply.47, u32[]{:T(128)S(6)} %multiply.48), kind=kLoop, calls=%fused_computation.169.clone.1 | loop fusion | bytes 18870284
  420.9 80.6 %dynamic-update-slice.4 = f32[7076352]{0:T(1024)} dynamic-update-slice(f32[7076352]{0:T(1024)} %get-tuple-element.446, f32[2358784]{0:T(1024)} %dynamic-slice_reduce_fusion.2, u32[]{:T(128)S(6)} %add.205) | dynamic-update-slice | bytes 18870276
  502.0 94.0 %dynamic-slice_reduce_fusion.2 = f32[2358784]{0:T(1024)} fusion(f32[]{:T(128)} %broadcast.171, f32[1,3,2358784]{2,1,0:T(4,128)} %get-tuple-element.453, u32[]{:T(128)S(6)} %multiply.47, u32[]{:T(128)S(6)} %multiply.48), kind=kLoop, calls=%fused_computation.169.clone.1 | loop fusion | bytes 18870284
  596.0 80.1 %dynamic-update-slice.4 = f32[7076352]{0:T(1024)} dynamic-update-slice(f32[7076352]{0:T(1024)} %get-tuple-element.446, f32[2358784]{0:T(1024)} %dynamic-slice_reduce_fusion.2, u32[]{:T(128)S(6)} %add.205) | dynamic-update-slice | bytes 18870276
  676.2 38.6 %reshape.309 = f32[3,512,4607]{2,1,0:T(8,128)} reshape(f32[7076352]{0:T(1024)} %get-tuple-element.197) | data formatting | bytes 56610816 | tf_op jit(solution)/shard_map/reshape | solution.py:46
  748.2 215.8 %while.28 = (s32[]{:T(128)}, bf16[4,512,1,3,64]{1,4,3,2,0:T(8,128)(2,1)S(1)}, f32[4,1,3,512,1]{3,2,4,1,0:T(4,128)S(1)}, bf16[4,1,3,512,4096]{4,3,2,1,0:T(8,128)(...) while((s32[]{:T(128)}, ...), condition=%wide.region_4.5_spmd, body=%wide.region_1.4_spmd.sunk | while | flops 1667332608 | bytes 142018672 | solution.py:122
  973.3 53.9 %reduce-scatter.4.cloned.1.call-done = f32[512,1,768]{2,0,1:T(8,128)} async-done(((f32[512,4,768]{2,0,1:T(8,128)}), f32[512,1,768]{2,0,1:T(8,128)}) %reduce-scatter.4.cloned.1.call-update) | async-done | bytes 1572880 | tf_op jit(solution)/shard_map/reduce_scatter | solution.py:129
  1177.3 29.6 %all-gather.6.cloned.1.call-done = bf16[512,4,768]{2,0,1:T(8,128)(2,1)} async-done(((bf16[512,1,768]{2,0,1:T(8,128)(2,1)}), bf16[512,4,768]{2,0,1:T(8,128)(2,1)}) %all-gather.6.cloned.1.call-update) | async-done | bytes 3145744 | tf_op jit(solution)/shard_map/all_gather | solution.py:216
  1248.3 290.6 %while.29 = (s32[]{:T(128)}, bf16[4,1,3,512,4096]{4,3,2,1,0:T(8,128)(2,1)}, bf16[4,512,1,3,64]{1,4,3,2,0:T(8,128)(2,1)}, bf16[4,512,1,3,64]{1,4,3,2,0:T(8,128)(2...) while((s32[]{:T(128)}, ...), condition=%wide.region_15.16_spmd, body=%wide.region_13.15_spmd.sunk | while | flops 2466445824 | bytes 194088064 | solution.py:244
  1259.8 26.2 multiply_reduce_fusion.4
  1286.0 25.2 bitcast_dynamic-update-slice_fusion.8
  1332.3 26.2 multiply_reduce_fusion.4
  1358.5 25.3 bitcast_dynamic-update-slice_fusion.8
  1404.9 26.2 multiply_reduce_fusion.4
  1431.1 25.4 bitcast_dynamic-update-slice_fusion.8
  1477.7 26.2 multiply_reduce_fusion.4
  1503.9 25.3 bitcast_dynamic-update-slice_fusion.8
  1560.3 22.3 fusion.58
  1602.6 196.6 %reduce-scatter.6.cloned.1.call-done = bf16[512,4,384]{0,2,1:T(8,128)(2,1)} async-done(((bf16[4096,4,384]{0,2,1:T(8,128)(2,1)}), bf16[512,4,384]{0,2,1:T(8,128)(2,1)}) %reduce-scatter.6.cloned.1.call-update) | async-done | bytes 1572880 | tf_op jit(solution)/shard_map/reduce_scatter | solution.py:255
  1855.8 36.1 %convert_reduce_fusion = f32[3,512,4096]{2,1,0:T(8,128)} fusion(bf16[4,1,3,512,4096]{4,3,2,1,0:T(8,128)(2,1)} %get-tuple-element.106), kind=kLoop, calls=%fused_computation.42 | loop fusion | flops 44040192 | bytes 75497472 | tf_op jit(solution)/shard_map/reduce_sum | solution.py:249
  1910.1 40.3 %reshape.339 = f32[7076352]{0:T(1024)} reshape(f32[3,512,4607]{2,1,0:T(8,128)} %pad.8) | data formatting | bytes 56610816
  1950.4 555.6 %while.31 = (u32[]{:T(128)}, f32[7076352]{0:T(1024)}, f32[1,3,2358784]{2,1,0:T(4,128)}, u32[]{}, u32[]{}, /*index=5*/u32[]{}, u32[]{}, u32[]{}) while((u32[]{:T(128)}, f32[7076352]{0:T(1024)}, f32[1,3,2358784]{2,1,0:T(4,128)}, u32[]{}, u32[]{}, /*index=5*/u32[]{}, u32[]{}, u32[]{}) %tuple.95), condition=%wide.cond.1, body=%wide.body.1.sunk | while | flops 9 | bytes 56611000
  1966.0 169.7 %dynamic-update-slice.5 = f32[1,3,2358784]{2,1,0:T(4,128)} dynamic-update-slice(f32[1,3,2358784]{2,1,0:T(4,128)} %get-tuple-element.527, f32[1,1,2358784]{2,1,0:T(1,128)} %reshape.342, u32[]{:T(128)S(6)} %multiply.51, u32[]{:T(128)S(6)} %multiply.53, u32[]{} %constant.247..sunk) | dynamic-update-slice | bytes 18870276
  2151.2 169.6 %dynamic-update-slice.5 = f32[1,3,2358784]{2,1,0:T(4,128)} dynamic-update-slice(f32[1,3,2358784]{2,1,0:T(4,128)} %get-tuple-element.527, f32[1,1,2358784]{2,1,0:T(1,128)} %reshape.342, u32[]{:T(128)S(6)} %multiply.51, u32[]{:T(128)S(6)} %multiply.53, u32[]{} %constant.247..sunk) | dynamic-update-slice | bytes 18870276
  2336.4 169.6 %dynamic-update-slice.5 = f32[1,3,2358784]{2,1,0:T(4,128)} dynamic-update-slice(f32[1,3,2358784]{2,1,0:T(4,128)} %get-tuple-element.527, f32[1,1,2358784]{2,1,0:T(1,128)} %reshape.342, u32[]{:T(128)S(6)} %multiply.51, u32[]{:T(128)S(6)} %multiply.53, u32[]{} %constant.247..sunk) | dynamic-update-slice | bytes 18870276
  2506.0 25.5 pad.9
  2580.6 43.5 %all-reduce.2 = (f32[768]{0:T(1024)}, f32[768]{0:T(1024)}, f32[32]{0:T(128)}) all-reduce(f32[768]{0:T(1024)S(1)} %get-tuple-element.203, f32[768]{0:T(1024)S(1)} %copy-done.35, f32[32]{0:T(128)S(1)} %copy-done.37), channel_id=1, replica_groups=mesh['head'=4,'seq'=8] {'head','seq'}, use_global_device_ids=true, to_apply=%region_20.21 | all-reduce | flops 1568 | bytes 12544 | tf_op jit(solution)/shard_map/psum | solution.py:289
  (251 shorter events, 829.6 us)
Async XLA Ops:
  7.2 724.8 %all-gather.8.cloned.1.call-start = ((), (), s32[]{:S(2)}) async-start(), calls=%async_computation.12 | async-start | bytes 7077888 | tf_op jit(solution)/shard_map/all_gather | solution.py:99
  59.5 672.6 %all-gather.10.cloned.1.call-start = ((), (), s32[]{:S(2)}) async-start(), calls=%async_computation.13 | async-start | bytes 7077888 | tf_op jit(solution)/shard_map/all_gather | solution.py:98
  67.5 959.6 %reduce-scatter.4.cloned.1.call-start = ((), (), s32[]{:S(2)}) async-start(), calls=%async_computation.7 | async-start | bytes 7864320 | tf_op jit(solution)/shard_map/reduce_scatter | solution.py:129
  748.2 215.8 %copy-start.13 = (bf16[192,768]{1,0:T(8,128)(2,1)S(1)}, bf16[192,768]{1,0:T(8,128)(2,1)}, u32[]{:S(2)}) copy-start(bf16[192,768]{1,0:T(8,128)(2,1)} %param.22) | copy-start | bytes 884740
  968.2 61.1 %copy-start.20 = (f32[768]{0:T(1024)S(1)}, f32[768]{0:T(1024)}, u32[]{:S(2)}) copy-start(f32[768]{0:T(1024)} %param.23) | copy-start | bytes 9220
  973.3 66.1 %copy-start.15 = (bf16[768,32]{0,1:T(8,128)(2,1)S(1)}, bf16[768,32]{0,1:T(8,128)(2,1)}, u32[]{:S(2)}) copy-start(bf16[768,32]{0,1:T(8,128)(2,1)} %param.24) | copy-start | bytes 147460
  973.3 66.1 %copy-start.38 = (f32[32]{0:T(128)S(1)}, f32[32]{0:T(128)}, u32[]{:S(2)}) copy-start(f32[32]{0:T(128)} %param.25) | copy-start | bytes 388
  1029.2 144.3 %copy-start.1 = (f32[512,1,768]{2,0,1:T(8,128)}, f32[512,1,768]{2,0,1:T(8,128)S(1)}, u32[]{:S(2)}) copy-start(f32[512,1,768]{2,0,1:T(8,128)S(1)} %get-tuple-element.263) | copy-start | bytes 4718596
  1029.3 144.2 %copy-start.24 = (f32[512]{0:T(512)}, f32[512]{0:T(512)S(1)}, u32[]{:S(2)}) copy-start(f32[512]{0:T(512)S(1)} %add_rsqrt_fusion.1) | copy-start | bytes 6148
  1034.4 31.7 %all-to-all-start = ((bf16[32,20,768]{2,1,0:T(8,128)(2,1)}), bf16[32,20,768]{2,1,0:T(8,128)(2,1)}, u32[]{:S(2)}, u32[]{:S(2)}) async-start(bf16[32,20,768]{2,1,0:T(8,128)(2,1)} %reshape.312), calls=%async_computation.1 | async-start | bytes 2359296 | tf_op jit(solution)/shard_map/all_to_all | solution.py:154
  1040.8 105.6 %copy-start.10 = (f32[512,32]{0,1:T(8,128)}, f32[512,32]{0,1:T(8,128)S(1)}, u32[]{:S(2)}) copy-start(f32[512,32]{0,1:T(8,128)S(1)} %get-tuple-element.276) | copy-start | bytes 196612
  1040.8 105.6 %copy-start.18 = (f32[512]{0:T(512)}, f32[512]{0:T(512)S(1)}, u32[]{:S(2)}) copy-start(f32[512]{0:T(512)S(1)} %get-tuple-element.275) | copy-start | bytes 6148
  1040.9 105.6 %copy-start.22 = (f32[512]{0:T(512)}, f32[512]{0:T(512)S(1)}, u32[]{:S(2)}) copy-start(f32[512]{0:T(512)S(1)} %fusion.119) | copy-start | bytes 6148
  1040.9 105.6 %copy-start.28 = (f32[512]{0:T(512)}, f32[512]{0:T(512)S(1)}, u32[]{:S(2)}) copy-start(f32[512]{0:T(512)S(1)} %select_reduce_fusion) | copy-start | bytes 6148
  1066.1 34.2 %all-to-all-start.2 = ((bf16[32,20,768]{2,1,0:T(8,128)(2,1)}), bf16[32,20,768]{2,1,0:T(8,128)(2,1)}, u32[]{:S(2)}, u32[]{:S(2)}) async-start(bf16[32,20,768]{2,1,0:T(8,128)(2,1)} %reshape.317), calls=%async_computation.3 | async-start | bytes 2359296 | tf_op jit(solution)/shard_map/all_to_all | solution.py:177
  1100.3 33.8 %all-to-all-start.1 = ((bf16[32,20,768]{2,1,0:T(8,128)(2,1)}), bf16[32,20,768]{2,1,0:T(8,128)(2,1)}, u32[]{:S(2)}, u32[]{:S(2)}) async-start(bf16[32,20,768]{2,1,0:T(8,128)(2,1)} %reshape.314), calls=%async_computation.2 | async-start | bytes 2359296 | tf_op jit(solution)/shard_map/all_to_all | solution.py:161
  1134.1 33.8 %all-to-all-start.3 = ((bf16[32,20,768]{2,1,0:T(8,128)(2,1)}), bf16[32,20,768]{2,1,0:T(8,128)(2,1)}, u32[]{:S(2)}, u32[]{:S(2)}) async-start(bf16[32,20,768]{2,1,0:T(8,128)(2,1)} %reshape.319), calls=%async_computation.4 | async-start | bytes 2359296 | tf_op jit(solution)/shard_map/all_to_all | solution.py:193
  1141.0 65.9 %all-gather.6.cloned.1.call-start = ((), (), s32[]{:S(2)}) async-start(), calls=%async_computation.8 | async-start | bytes 3932160 | tf_op jit(solution)/shard_map/all_gather | solution.py:216
  1173.5 45.4 %copy-start.32 = (f32[512]{0:T(512)}, f32[512]{0:T(512)S(1)}, u32[]{:S(2)}) copy-start(f32[512]{0:T(512)S(1)} %broadcast_multiply_fusion.1) | copy-start | bytes 6148
  1177.2 41.7 %copy-start.14 = (bf16[192,768]{1,0:T(8,128)(2,1)S(1)}, bf16[192,768]{1,0:T(8,128)(2,1)}, u32[]{:S(2)}) copy-start(bf16[192,768]{1,0:T(8,128)(2,1)} %param.22) | copy-start | bytes 884740
  1177.2 622.0 %reduce-scatter.6.cloned.1.call-start = ((), (), s32[]{:S(2)}) async-start(), calls=%async_computation.9 | async-start | bytes 14155776 | tf_op jit(solution)/shard_map/reduce_scatter | solution.py:255
  1593.0 977.1 %all-reduce.9.cloned.1.call-start = ((), (), s32[]{:S(2)}) async-start(), calls=%async_computation.14 | async-start | bytes 2359296 | tf_op jit(solution)/shard_map/psum | solution.py:285
  1827.1 747.4 %reduce-scatter.8.cloned.1.call-start = ((), (), s32[]{:S(2)}) async-start(), calls=%async_computation.10 | async-start | bytes 3932160 | tf_op jit(solution)/shard_map/reduce_scatter | solution.py:279
  1831.5 792.7 %all-reduce.7.cloned.1.call-start = ((), (), s32[]{:S(2)}) async-start(), calls=%async_computation.11 | async-start | bytes 196608 | tf_op jit(solution)/shard_map/psum | solution.py:289
  2531.5 20.2 copy-start.40
  2531.5 43.0 %copy-start.27 = (f32[768]{0:T(1024)S(1)}, f32[768]{0:T(1024)}, u32[]{:S(2)}) copy-start(f32[768]{0:T(1024)} %param.19) | copy-start | bytes 9220
  2531.5 43.0 %copy-start.34 = (f32[512,1]{0,1:T(1,128)S(1)}, f32[512,1]{0,1:T(1,128)}, u32[]{:S(2)}) copy-start(f32[512,1]{0,1:T(1,128)} %constant_dynamic-slice_fusion) | copy-start | bytes 6148
  2551.6 25.2 copy-start.2
  2551.6 25.2 copy-start.9
  2551.6 25.2 copy-start.21
  2551.6 25.2 copy-start.25
  2551.6 25.2 copy-start.33
  (23 other events, 189.4 us)
Sparse Core Ops, SparseCore 0:
  59.6 98.1 all-gather.7
  160.5 98.1 all-gather.9
  967.9 59.1 reduce-scatter.3
  1177.3 29.5 all-gather.5
  1593.2 206.0 reduce-scatter.5
  1827.3 80.7 all-reduce.8
  1910.5 37.5 reduce-scatter.7
  1955.3 122.3 all-reduce.6
where the time goes:
time: 2670 us; the launch traced here: 2630 us
  local copies, waits for them, and re-layouts  1460 us (55%)
  matrix products  445 us (17%)
  waiting for transfers between devices  329 us (12%)
  other arithmetic  295 us (11%)
  blocking collectives  60.8 us (2%)
  starting transfers between devices  26.7 us (1%)
    unnamed x110, local copies, waits for them, and re-layouts  1210 us
    reduce_scatter x1, waiting for transfers between devices, local(): lax.psum_scatter(jnp.concatenate([grad_k.reshape(count, seqs, hidden_widt...  197 us
    dot_general x8, matrix products, block_scores(): jnp.einsum('ibhd,jbhd->bhij', query, keys, preferred_element_type=jnp.flo...  171 us
    dynamic_update_slice x12, other arithmetic, local(): lax.map(attend_block, (group_query, group_keys, group_vals))  158 us
    reduce_scatter x1, waiting for transfers between devices, local(): lax.psum_scatter(partial_value, 'head', scatter_dimension=1, tiled=True)  53.9 us
  transfers between devices with their start and end apart: 12, of which 7 were waited for; matrix products, arithmetic and copies ran while one was open for 56% of the time, Pallas kernels for 0%

commit v1 on v0

v1 whole, which is shorter than its diff:
```python
import functools
import math

import jax
import jax.numpy as jnp
from jax import lax
from jax.experimental import pallas as pl
from jax.experimental.pallas import tpu as pltpu
from jax.sharding import PartitionSpec as P

F32 = jnp.float32
BF16 = jnp.bfloat16
LOG2E = math.log2(math.e)
MB = 1024 * 1024
eps = 1e-06
HIGH = lax.Precision.HIGHEST

def nt(a,b): return lax.dot_general(a,b,(((1,),(1,)),((),())),preferred_element_type=F32)
def nn(a,b): return jnp.dot(a,b,preferred_element_type=F32)

def build_strip(win_ref, strip, length, qlen):
    tiles = (length + qlen)//128 - 1
    def one(d, _):
        start = pl.multiple_of(length + qlen - 256 - 128*d, 128)
        u = jnp.broadcast_to(win_ref[0, :, pl.ds(start, 256)], (128, 256))
        strip[pl.ds(pl.multiple_of(d*128,128), 128), :] = pltpu.roll(u, 0, 1, stride=1, stride_axis=0)[:, 128:]
        return 0
    lax.fori_loop(0, tiles, one, 0)

def split3(x):
    hi = x.astype(BF16); r = x - hi.astype(F32)
    mid = r.astype(BF16); lo = (r - mid.astype(F32)).astype(BF16)
    return hi, mid, lo

def rows16(x, n):
    hi, mid, lo = split3(x)
    at = lax.broadcasted_iota(jnp.int32, (16, n), 0)
    z = jnp.zeros((16, n), F32)
    out = jnp.where(at == 0, hi.astype(F32), jnp.where(at == 1, mid.astype(F32), jnp.where(at == 2, lo.astype(F32), z)))
    return out.astype(BF16)

def fwd_kernel(length, qlen, hd, bi, bj, win_ref, q_ref, k_ref, v_ref, out_ref, lse_ref, strip, kaug, qaug, vaug):
    build_strip(win_ref, strip, length, qlen)
    scaled = q_ref[0].astype(F32) * (hd ** -0.5 * LOG2E)
    hi = scaled.astype(BF16)
    qaug[:hd, :] = hi
    qaug[hd:, :] = (scaled - hi.astype(F32)).astype(BF16)
    kk = k_ref[0, 0].T
    kaug[:, :hd] = kk
    kaug[:, hd:] = kk
    vaug[:hd, :] = v_ref[0, 0]
    vaug[hd:, :] = jnp.ones((16, length), BF16)
    def iblock(ib, _):
        i0 = pl.multiple_of(ib*bi, bi)
        q = qaug[:, pl.ds(i0, bi)]
        def jblock(jb, carry):
            m, acc = carry
            j0 = pl.multiple_of(jb*bj, bj)
            s = nn(kaug[pl.ds(j0, bj), :], q)
            bias = [strip[pl.ds(pl.multiple_of(j0 - i0 - 128*c + qlen - 128, 128), bj), :] for c in range(bi//128)]
            s = s + jnp.concatenate(bias, axis=1)
            mn = jnp.maximum(m, jnp.max(s, axis=0, keepdims=True))
            p = jnp.exp2(s - mn).astype(BF16)
            acc = acc * jnp.exp2(m - mn) + nn(vaug[:, pl.ds(j0, bj)], p)
            return mn, acc
        m, acc = lax.fori_loop(0, length//bj, jblock, (jnp.full((1, bi), -1e30, F32), jnp.zeros((hd+16, bi), F32)))
        l = acc[hd:hd+1]
        out_ref[0, :, pl.ds(i0, bi)] = (acc[:hd] / l).astype(BF16)
        lse_ref[0, :, pl.ds(i0, bi)] = m + jnp.log2(l)
        return 0
    lax.fori_loop(0, qlen//bi, iblock, 0)

def attn_fwd(win, qT, kvT, bi=512, bj=512):
    heads, hd, qlen = qT.shape
    length = kvT.shape[3]
    tiles = (length+qlen)//128-1
    return pl.pallas_call(
        functools.partial(fwd_kernel, length, qlen, hd, bi, bj),
        grid=(heads,),
        out_shape=[jax.ShapeDtypeStruct((heads, hd, qlen), BF16), jax.ShapeDtypeStruct((heads, 1, qlen), F32)],
        in_specs=[pl.BlockSpec((1,1,length+qlen), lambda n:(n,0,0)), pl.BlockSpec((1,hd,qlen), lambda n:(n,0,0)),
            pl.BlockSpec((1,1,hd,length), lambda n:(n,1,0,0)), pl.BlockSpec((1,1,hd,length), lambda n:(n,2,0,0))],
        out_specs=[pl.BlockSpec((1,hd,qlen), lambda n:(n,0,0)), pl.BlockSpec((1,1,qlen), lambda n:(n,0,0))],
        scratch_shapes=[pltpu.VMEM((tiles*128,128),F32), pltpu.VMEM((length,2*hd),BF16), pltpu.VMEM((2*hd,qlen),BF16), pltpu.VMEM((hd+16,length),BF16)],
        compiler_params=pltpu.CompilerParams(vmem_limit_bytes=56*MB),
        name="attn_forward",
    )(win, qT, kvT, kvT)

def bwd_kernel(length, qlen, hd, bi, bj, win_ref, q_ref, k_ref, v_ref, o_ref, do_ref, lse_ref,
               dq_ref, dkv_ref, dwin_ref, strip, dstrip, kaug, qaug, vaug, doaug, dk_acc, dv_acc, dwide):
    build_strip(win_ref, strip, length, qlen)
    tiles = (length + qlen)//128 - 1
    scale = hd ** -0.5
    scaled = q_ref[0].astype(F32) * (scale * LOG2E)
    hi = scaled.astype(BF16)
    qaug[:hd, :] = hi
    qaug[hd:2*hd, :] = (scaled - hi.astype(F32)).astype(BF16)
    qaug[2*hd:2*hd+16, :] = rows16(-lse_ref[0], qlen)
    qaug[2*hd+16:, :] = jnp.zeros((2*hd-16, qlen), BF16)
    kk = k_ref[0, 0].T
    kaug[:, :hd] = kk
    kaug[:, hd:2*hd] = kk
    kaug[:, 2*hd:] = jnp.ones((length, 2*hd), BF16)
    vaug[:, :hd] = v_ref[0, 0].T
    vaug[:, hd:] = jnp.ones((length, hd), BF16)
    do = do_ref[0]
    delta = jnp.sum(do.astype(F32) * o_ref[0].astype(F32), axis=0, keepdims=True)
    doaug[:hd, :] = do
    doaug[hd:hd+16, :] = rows16(-delta, qlen)
    doaug[hd+16:, :] = jnp.zeros((hd-16, qlen), BF16)
    dstrip[...] = jnp.zeros_like(dstrip)
    dk_acc[...] = jnp.zeros_like(dk_acc)
    dv_acc[...] = jnp.zeros_like(dv_acc)
    def iblock(ib, _):
        i0 = pl.multiple_of(ib*bi, bi)
        qa = qaug[:, pl.ds(i0, bi)]
        da = doaug[:, pl.ds(i0, bi)]
        q = q_ref[0, :, pl.ds(i0, bi)]
        d = do_ref[0, :, pl.ds(i0, bi)]
        def jblock(jb, dq):
            j0 = pl.multiple_of(jb*bj, bj)
            s = nn(kaug[pl.ds(j0, bj), :], qa)
            at = [pl.ds(pl.multiple_of(j0 - i0 - 128*c + qlen - 128, 128), bj) for c in range(bi//128)]
            p = jnp.exp2(s + jnp.concatenate([strip[a, :] for a in at], axis=1))
            dp = nn(vaug[pl.ds(j0, bj), :], da)
            ds = p * dp
            for c, a in enumerate(at):
                dstrip[a, :] += ds[:, c*128:(c+1)*128]
            dsl = ds.astype(BF16)
            dv_acc[:, pl.ds(j0, bj)] += nt(d, p.astype(BF16))
            dk_acc[:, pl.ds(j0, bj)] += nt(q, dsl)
            return dq + nn(k_ref[0, 0, :, pl.ds(j0, bj)], dsl)
        dq = lax.fori_loop(0, length//bj, jblock, jnp.zeros((hd, bi), F32))
        dq_ref[0, :, pl.ds(i0, bi)] = (dq * scale).astype(BF16)
        return 0
    lax.fori_loop(0, qlen//bi, iblock, 0)
    dkv_ref[0, 0] = (dk_acc[...] * scale).astype(BF16)
    dkv_ref[0, 1] = dv_acc[...].astype(BF16)
    total = length + qlen
    dwide[...] = jnp.zeros_like(dwide)
    def one(d, _):
        start = pl.multiple_of(total - 256 - 128*d, 128)
        t = dstrip[pl.ds(pl.multiple_of(d*128,128), 128), :]
        gathered = jnp.zeros((8, 256), F32)
        for a in range(16):
            wide = jnp.concatenate([jnp.zeros((8,128),F32), t[8*a:8*a+8]], axis=1)
            gathered = gathered + (pltpu.roll(wide, 256 - 8*a, 1) if a else wide)
        dwide[:, pl.ds(start, 256)] += gathered
        return 0
    lax.fori_loop(0, tiles, one, 0)
    x = dwide[...]
    at = lax.broadcasted_iota(jnp.int32, x.shape, 0)
    for bit in (1, 2, 4):
        x = jnp.where((at & bit) != 0, pltpu.roll(x, total - bit, 1), x)
    dwin_ref[0] = jnp.sum(x, axis=0, keepdims=True)

def attn_bwd(win, qT, kvT, oT, doT, lse, bi=512, bj=512):
    heads, hd, qlen = qT.shape
    length = kvT.shape[3]
    tiles = (length+qlen)//128-1
    q_spec = pl.BlockSpec((1,hd,qlen), lambda n:(n,0,0))
    w_spec = pl.BlockSpec((1,1,length+qlen), lambda n:(n,0,0))
    return pl.pallas_call(
        functools.partial(bwd_kernel, length, qlen, hd, bi, bj),
        grid=(heads,),
        out_shape=[jax.ShapeDtypeStruct((heads, hd, qlen), BF16), jax.ShapeDtypeStruct((heads, 2, hd, length), BF16), jax.ShapeDtypeStruct((heads,1,length+qlen),F32)],
        in_specs=[w_spec, q_spec,
            pl.BlockSpec((1,1,hd,length), lambda n:(n,1,0,0)), pl.BlockSpec((1,1,hd,length), lambda n:(n,2,0,0)),
            q_spec, q_spec, pl.BlockSpec((1,1,qlen), lambda n:(n,0,0))],
        out_specs=[q_spec, pl.BlockSpec((1,2,hd,length), lambda n:(n,0,0,0)), w_spec],
        scratch_shapes=[pltpu.VMEM((tiles*128,128),F32), pltpu.VMEM((tiles*128,128),F32), pltpu.VMEM((length,4*hd),BF16), pltpu.VMEM((4*hd,qlen),BF16),
            pltpu.VMEM((length,2*hd),BF16), pltpu.VMEM((2*hd,qlen),BF16), pltpu.VMEM((hd,length),F32), pltpu.VMEM((hd,length),F32), pltpu.VMEM((8,length+qlen),F32)],
        compiler_params=pltpu.CompilerParams(vmem_limit_bytes=56*MB),
        name="attn_backward",
    )(win, qT, kvT, kvT, oT, doT, lse)


MESH = pl.DeviceIdType.MESH


def greet(peers):
    barrier = pltpu.get_barrier_semaphore()
    for peer in peers:
        pl.semaphore_signal(barrier, inc=1, device_id=peer, device_id_type=MESH)
    pl.semaphore_wait(barrier, len(peers))


def remote(source, target, send, recv, peer):
    return pltpu.make_async_remote_copy(
        src_ref=source,
        dst_ref=target,
        send_sem=send,
        recv_sem=recv,
        device_id=peer,
        device_id_type=MESH,
    )


def start_any(source, target, send, recv, peer, is_self):
    @pl.when(is_self)
    def _():
        pltpu.make_async_copy(source, target, recv).start()

    @pl.when(jnp.logical_not(is_self))
    def _():
        remote(source, target, send, recv, peer).start()


def wait_any(source, target, send, recv, peer, is_self):
    remote(source, target, send, recv, peer).wait_recv()

    @pl.when(jnp.logical_not(is_self))
    def _():
        remote(source, target, send, recv, peer).wait_send()


def gather_kernel(n_seq, ways, tsd, piece, rows_in, out, own_sem, a_send, a_recv, p_send, p_recv):
    head, seq = lax.axis_index("head"), lax.axis_index("seq")
    half = lax.rem(seq, ways)
    cross, sibling, beside = (head ^ 2, seq), (head ^ 1, seq), (head, seq ^ 1)
    greet([(head, seq ^ k) for k in range(1, n_seq)] + [cross, sibling])

    def rows_of(k, of_head, of_half):
        at = (seq ^ k) * tsd + (of_head * ways + of_half) * piece
        return out.at[pl.ds(pl.multiple_of(at, piece), piece), :]

    first = []
    for k in range(n_seq):
        to = seq ^ k
        to_half = lax.rem(to, ways)
        source = rows_in.at[lax.div(to, ways), pl.ds(pl.multiple_of(to_half * piece, piece), piece), :]
        at = seq * tsd + (head * ways + to_half) * piece
        target = out.at[pl.ds(pl.multiple_of(at, piece), piece), :]
        if k == 0:
            copy = pltpu.make_async_copy(source, target, own_sem)
        else:
            copy = remote(source, target, a_send.at[k], a_recv.at[k], (head, to))
        copy.start()
        first.append(copy)

    started = []

    def send(kind, k, of_head, of_half, peer, recv_k=None):
        ref = rows_of(k, of_head, of_half)
        copy = remote(ref, ref, p_send.at[kind, k], p_recv.at[kind, k if recv_k is None else recv_k], peer)
        copy.start()
        started.append(copy)

    def arrived(kind, k, of_head, of_half):
        ref = rows_of(k, of_head, of_half)
        remote(ref, ref, p_send.at[kind, k], p_recv.at[kind, k], cross).wait_recv()

    def stage_own(k):
        if k == 0:
            first[0].wait()
        else:
            ref = rows_of(k, head, half)
            remote(ref, ref, a_send.at[k], a_recv.at[k], cross).wait_recv()
        send(0, k, head, half, cross)
        send(1, k, head, half, beside, k ^ 1)
        send(3, k, head, half, sibling)

    def stage_pass(k):
        arrived(0, k, head ^ 2, half)
        arrived(1, k, head, half ^ 1)
        odd = lax.rem(seq ^ k, 2)
        to_head = jnp.where(odd == 1, head ^ 2, head)
        to_seq = jnp.where(odd == 1, seq, seq ^ 1)
        of_head = jnp.where(odd == 1, head, head ^ 2)
        of_half = jnp.where(odd == 1, half ^ 1, half)
        send(2, k, of_head, of_half, (to_head, to_seq), jnp.where(odd == 1, k, k ^ 1))
        send(4, k, head ^ 2, half, sibling)
        send(5, k, head, half ^ 1, sibling)

    def stage_last(k):
        arrived(2, k, head ^ 2, half ^ 1)
        send(6, k, head ^ 2, half ^ 1, sibling)

    for step in range(n_seq + 2):
        if step < n_seq:
            stage_own(step)
        if 1 <= step <= n_seq:
            stage_pass(step - 1)
        if 2 <= step:
            stage_last(step - 2)
    for k in range(n_seq):
        arrived(3, k, head ^ 1, half)
        arrived(4, k, head ^ 3, half)
        arrived(5, k, head ^ 1, half ^ 1)
        arrived(6, k, head ^ 3, half ^ 1)
    for copy in first[1:] + started:
        copy.wait_send()


def gather_rows(rows_in, n_seq, ways, tsd):
    width = rows_in.shape[2]
    piece = rows_in.shape[1] // ways
    return pl.pallas_call(
        functools.partial(gather_kernel, n_seq, ways, tsd, piece),
        out_shape=jax.ShapeDtypeStruct((n_seq * tsd, width), rows_in.dtype),
        in_specs=[pl.BlockSpec(memory_space=pl.ANY)],
        out_specs=pl.BlockSpec(memory_space=pl.ANY),
        scratch_shapes=[
            pltpu.SemaphoreType.DMA,
            pltpu.SemaphoreType.DMA((n_seq,)),
            pltpu.SemaphoreType.DMA((n_seq,)),
            pltpu.SemaphoreType.DMA((7, n_seq)),
            pltpu.SemaphoreType.DMA((7, n_seq)),
        ],
        compiler_params=pltpu.CompilerParams(collective_id=1, has_side_effects=True),
        name="gather_rows",
    )(rows_in)


def to_residual_kernel(own, ways, seqs, n_head, tsd, source, out, send, recv):
    head, seq = lax.axis_index("head"), lax.axis_index("seq")
    batch, half = lax.div(seq, ways), lax.rem(seq, ways)
    to_head = lax.div(batch, own)
    inner = lax.rem(batch, own)
    mine_half = lax.div(seq, seqs)
    mine_at = lax.rem(seq, seqs)
    greet_both(own, ways, seqs, n_head, head, seq)
    calls = []
    for k in range(seqs):
        j = lax.rem(head * own + inner + k, seqs)
        to_seq = half * seqs + j
        is_self = jnp.logical_and(to_head == head, to_seq == seq)
        piece = source.at[:, pl.ds(pl.multiple_of(j * tsd, tsd), tsd)]
        args = (piece, out.at[inner, head], send.at[k], recv.at[k], (to_head, to_seq), is_self)
        start_any(*args)
        calls.append(args)
    for k, args in enumerate(calls):
        number = lax.rem(mine_at - k + seqs, seqs)
        from_head, from_inner = lax.div(number, own), lax.rem(number, own)
        landed = out.at[from_inner, from_head]
        remote(landed, landed, send.at[k], recv.at[k], (to_head, seq)).wait_recv()
        piece, target, sem, arrival, peer, is_self = args

        @pl.when(jnp.logical_not(is_self))
        def _():
            remote(piece, target, sem, arrival, peer).wait_send()


def greet_both(own, ways, seqs, n_head, head, seq):
    batch, half = lax.div(seq, ways), lax.rem(seq, ways)
    inner = lax.rem(batch, own)
    mine_half, mine_at = lax.div(seq, seqs), lax.rem(seq, seqs)
    barrier = pltpu.get_barrier_semaphore()
    for k in range(seqs):
        j = lax.rem(head * own + inner + k, seqs)
        number = lax.rem(mine_at - k + seqs, seqs)
        source_seq = (head * own + lax.rem(number, own)) * ways + mine_half
        for peer in ((lax.div(batch, own), half * seqs + j), (lax.div(number, own), source_seq)):
            pl.semaphore_signal(barrier, inc=1, device_id=peer, device_id_type=MESH)
    pl.semaphore_wait(barrier, 2 * seqs)


def to_residual(source, own, ways, seqs, n_head, tsd):
    rows = source.shape[0]
    return pl.pallas_call(
        functools.partial(to_residual_kernel, own, ways, seqs, n_head, tsd),
        out_shape=jax.ShapeDtypeStruct((own, n_head, rows, tsd), source.dtype),
        in_specs=[pl.BlockSpec(memory_space=pl.ANY)],
        out_specs=pl.BlockSpec(memory_space=pl.ANY),
        scratch_shapes=[pltpu.SemaphoreType.DMA((seqs,)), pltpu.SemaphoreType.DMA((seqs,))],
        compiler_params=pltpu.CompilerParams(collective_id=2, has_side_effects=True),
        name="to_residual",
    )(source)


def to_attention_kernel(own, ways, seqs, n_head, tsd, source, out, send, recv):
    head, seq = lax.axis_index("head"), lax.axis_index("seq")
    batch, half = lax.div(seq, ways), lax.rem(seq, ways)
    inner = lax.rem(batch, own)
    mine_half, mine_at = lax.div(seq, seqs), lax.rem(seq, seqs)
    greet_both(own, ways, seqs, n_head, head, seq)
    lanes = pl.ds(pl.multiple_of(mine_at * tsd, tsd), tsd)
    calls = []
    for k in range(seqs):
        number = lax.rem(mine_at - k + seqs, seqs)
        to_head, to_inner = lax.div(number, own), lax.rem(number, own)
        to_seq = (head * own + to_inner) * ways + mine_half
        is_self = jnp.logical_and(to_head == head, to_seq == seq)
        args = (source.at[to_inner, to_head], out.at[:, lanes], send.at[k], recv.at[k], (to_head, to_seq), is_self)
        start_any(*args)
        calls.append(args)
    for k, args in enumerate(calls):
        j = lax.rem(head * own + inner + k, seqs)
        landed = out.at[:, pl.ds(pl.multiple_of(j * tsd, tsd), tsd)]
        remote(landed, landed, send.at[k], recv.at[k], (head ^ 1, seq)).wait_recv()
        piece, target, sem, arrival, peer, is_self = args

        @pl.when(jnp.logical_not(is_self))
        def _():
            remote(piece, target, sem, arrival, peer).wait_send()


def to_attention(source, own, ways, seqs, n_head, tsd):
    rows = source.shape[2]
    return pl.pallas_call(
        functools.partial(to_attention_kernel, own, ways, seqs, n_head, tsd),
        out_shape=jax.ShapeDtypeStruct((rows, seqs * tsd), source.dtype),
        in_specs=[pl.BlockSpec(memory_space=pl.ANY)],
        out_specs=pl.BlockSpec(memory_space=pl.ANY),
        scratch_shapes=[pltpu.SemaphoreType.DMA((seqs,)), pltpu.SemaphoreType.DMA((seqs,))],
        compiler_params=pltpu.CompilerParams(collective_id=3, has_side_effects=True),
        name="to_attention",
    )(source)


def exchange_kernel(n_head, n_seq, source, out, own_sem, send, recv):
    me = lax.axis_index("head") * n_seq + lax.axis_index("seq")
    devices = n_head * n_seq

    def place(k):
        other = me ^ k
        return lax.div(other, n_seq), lax.rem(other, n_seq)

    greet([place(k) for k in range(1, devices)])
    own = pltpu.make_async_copy(source.at[me], out.at[me], own_sem)
    own.start()
    copies = []
    for k in range(1, devices):
        copy = remote(source.at[me ^ k], out.at[me], send.at[k], recv.at[k], place(k))
        copy.start()
        copies.append(copy)
    own.wait()
    for k, copy in enumerate(copies, 1):
        landed = out.at[me ^ k]
        remote(landed, landed, send.at[k], recv.at[k], place(k)).wait_recv()
        copy.wait_send()


def exchange(source, n_head, n_seq, collective_id, name):
    devices = n_head * n_seq
    return pl.pallas_call(
        functools.partial(exchange_kernel, n_head, n_seq),
        out_shape=jax.ShapeDtypeStruct(source.shape, source.dtype),
        in_specs=[pl.BlockSpec(memory_space=pl.ANY)],
        out_specs=pl.BlockSpec(memory_space=pl.ANY),
        scratch_shapes=[
            pltpu.SemaphoreType.DMA,
            pltpu.SemaphoreType.DMA((devices,)),
            pltpu.SemaphoreType.DMA((devices,)),
        ],
        compiler_params=pltpu.CompilerParams(collective_id=collective_id, has_side_effects=True),
        name=name,
    )(source)


def scatter_kernel(own, ways, groups, parts, out, got1, got2, got3, sum1, sum2, sum3, send, recv, last_send, last_recv):
    head, seq = lax.axis_index("head"), lax.axis_index("seq")
    core, x = lax.rem(head, 2), lax.div(head, 2)
    batch, y = lax.div(seq, ways), lax.rem(seq, ways)
    sibling, cross, beside = (head ^ 1, seq), (head ^ 2, seq), (head, seq ^ 1)
    to_head, inner = lax.div(batch, own), lax.rem(batch, own)
    n_seq = 8 * groups

    def home(v):
        return core * 4 * groups + v * 4 + x * 2 + y

    barrier = pltpu.get_barrier_semaphore()
    peers = [sibling, cross, beside]
    for v in range(groups):
        peers.append((to_head, home(v)))
    from_core, from_v = lax.div(seq, 4 * groups), lax.rem(lax.div(seq, 4), groups)
    from_x, from_y = lax.rem(lax.div(seq, 2), 2), lax.rem(seq, 2)
    for i in range(own):
        peers.append((from_x * 2 + from_core, (head * own + i) * ways + from_y))
    for peer in peers:
        pl.semaphore_signal(barrier, inc=1, device_id=peer, device_id_type=MESH)
    pl.semaphore_wait(barrier, len(peers))

    pending = []

    def go(stage, v, slot, source, target, peer):
        copy = remote(source, target, send.at[stage, v, slot], recv.at[stage, v, slot], peer)
        copy.start()
        pending.append(copy)

    def landed(stage, v, slot, target):
        remote(target, target, send.at[stage, v, slot], recv.at[stage, v, slot], sibling).wait_recv()

    order = [(1, 0, 0), (0, 1, 1), (1, 1, 0), (1, 1, 1), (0, 1, 0), (1, 0, 1), (0, 0, 0), (0, 0, 1)]
    for v in range(groups):
        for slot, (dx, dy, w) in enumerate(order):
            go(0, v, slot, parts.at[1 - core, v, x ^ dx, y ^ dy, w], got1.at[v, slot], sibling)
    for v in range(groups):
        for slot, (dx, dy, w) in enumerate(order):
            landed(0, v, slot, got1.at[v, slot])
            sum1[v, slot] = (
                parts[core, v, x ^ dx, y ^ dy, w].astype(jnp.float32) + got1[v, slot].astype(jnp.float32)
            ).astype(sum1.dtype)
            if w == 0 and dx == 1:
                go(1, v, 1 - dy, sum1.at[v, slot], got2.at[v, 1 - dy], cross)
            if w == 1 and dy == 1:
                go(1, v, 2 + 1 - dx, sum1.at[v, slot], got2.at[v, 2 + 1 - dx], beside)
    kept = {0: (0, 1, 0), 1: (0, 0, 0), 2: (1, 0, 1), 3: (0, 0, 1)}
    for v in range(groups):
        for slot in (0, 2, 1, 3):
            landed(1, v, slot, got2.at[v, slot])
            sum2[v, slot] = (
                sum1[v, order.index(kept[slot])].astype(jnp.float32) + got2[v, slot].astype(jnp.float32)
            ).astype(sum2.dtype)
            if slot == 0:
                go(2, v, 0, sum2.at[v, 0], got3.at[v, 0], beside)
            if slot == 2:
                go(2, v, 1, sum2.at[v, 2], got3.at[v, 1], cross)
    last = []
    for v in range(groups):
        for w in (0, 1):
            landed(2, v, w, got3.at[v, w])
            sum3[v, w] = (
                sum2[v, 1 + 2 * w].astype(jnp.float32) + got3[v, w].astype(jnp.float32)
            ).astype(sum3.dtype)
        is_self = jnp.logical_and(to_head == head, home(v) == seq)
        args = (sum3.at[v], out.at[inner], last_send.at[v], last_recv.at[inner], (to_head, home(v)), is_self)
        start_any(*args)
        last.append(args)
    for i in range(own):
        remote(out.at[i], out.at[i], last_send.at[0], last_recv.at[i], sibling).wait_recv()
    for piece, target, sem, arrival, peer, is_self in last:

        @pl.when(jnp.logical_not(is_self))
        def _():
            remote(piece, target, sem, arrival, peer).wait_send()

    for copy in pending:
        copy.wait_send()


def scatter_sums(parts, own, ways, n_seq, tsd):
    width = parts.shape[-1]
    groups = n_seq // 8
    rows = tsd // 2
    dtype = parts.dtype
    shaped = parts.reshape(2, groups, 2, 2, 2, rows, width)
    out = pl.pallas_call(
        functools.partial(scatter_kernel, own, ways, groups),
        out_shape=jax.ShapeDtypeStruct((own, 2, rows, width), dtype),
        in_specs=[pl.BlockSpec(memory_space=pltpu.VMEM)],
        out_specs=pl.BlockSpec(memory_space=pltpu.VMEM),
        scratch_shapes=[
            pltpu.VMEM((groups, 8, rows, width), dtype),
            pltpu.VMEM((groups, 4, rows, width), dtype),
            pltpu.VMEM((groups, 2, rows, width), dtype),
            pltpu.VMEM((groups, 8, rows, width), dtype),
            pltpu.VMEM((groups, 4, rows, width), dtype),
            pltpu.VMEM((groups, 2, rows, width), dtype),
            pltpu.SemaphoreType.DMA((3, groups, 8)),
            pltpu.SemaphoreType.DMA((3, groups, 8)),
            pltpu.SemaphoreType.DMA((groups,)),
            pltpu.SemaphoreType.DMA((own,)),
        ],
        compiler_params=pltpu.CompilerParams(
            collective_id=6, has_side_effects=True, vmem_limit_bytes=48 * MB
        ),
        name="scatter_sums",
    )(shaped)
    return out.reshape(own, tsd, width)


def reduce_kernel(n_head, n_seq, parts, small, out, small_out, got, own, got_small, own_small, sends, recvs, small_sends, small_recvs):
    head, seq = lax.axis_index("head"), lax.axis_index("seq")
    me = head * n_seq + seq
    devices = n_head * n_seq

    def place(k):
        other = me ^ k
        return lax.div(other, n_seq), lax.rem(other, n_seq)

    greet([place(k) for k in range(1, devices)])
    waits = []
    for k in range(1, devices):
        copy = remote(small.at[me ^ k], got_small.at[k], small_sends.at[0, k], small_recvs.at[0, k], place(k))
        copy.start()
        waits.append(copy)
    for k in range(1, n_seq):
        copy = remote(parts.at[seq ^ k], got.at[k], sends.at[0, k], recvs.at[0, k], (head, seq ^ k))
        copy.start()
        waits.append(copy)
    total = small[me]
    for k in range(1, devices):
        remote(got_small.at[k], got_small.at[k], small_sends.at[0, k], small_recvs.at[0, k], place(k)).wait_recv()
        total = total + got_small[k]
    own_small[...] = total
    small_out[me] = total
    for k in range(1, devices):
        copy = remote(own_small, small_out.at[me], small_sends.at[1, k], small_recvs.at[1, k], place(k))
        copy.start()
        waits.append(copy)
    total = parts[seq].astype(jnp.float32)
    for k in range(1, n_seq):
        remote(got.at[k], got.at[k], sends.at[0, k], recvs.at[0, k], (head, seq ^ k)).wait_recv()
        total = total + got[k].astype(jnp.float32)
    own[...] = total.astype(own.dtype)
    out[seq] = total.astype(own.dtype)
    for k in range(1, n_seq):
        copy = remote(own, out.at[seq], sends.at[1, k], recvs.at[1, k], (head, seq ^ k))
        copy.start()
        waits.append(copy)
    for k in range(1, devices):
        landed = small_out.at[me ^ k]
        remote(landed, landed, small_sends.at[1, k], small_recvs.at[1, k], place(k)).wait_recv()
    for k in range(1, n_seq):
        landed = out.at[seq ^ k]
        remote(landed, landed, sends.at[1, k], recvs.at[1, k], (head, seq ^ k)).wait_recv()
    for copy in waits:
        copy.wait_send()


def reduce_weights(parts, small, n_head, n_seq):
    devices = n_head * n_seq
    rows, width = parts.shape[1:]
    whole = pl.BlockSpec(memory_space=pltpu.VMEM)
    return pl.pallas_call(
        functools.partial(reduce_kernel, n_head, n_seq),
        out_shape=[
            jax.ShapeDtypeStruct(parts.shape, parts.dtype),
            jax.ShapeDtypeStruct(small.shape, small.dtype),
        ],
        in_specs=[whole, whole],
        out_specs=[whole, whole],
        scratch_shapes=[
            pltpu.VMEM((n_seq, rows, width), parts.dtype),
            pltpu.VMEM((rows, width), parts.dtype),
            pltpu.VMEM((devices, 8, 128), small.dtype),
            pltpu.VMEM((8, 128), small.dtype),
            pltpu.SemaphoreType.DMA((2, n_seq)),
            pltpu.SemaphoreType.DMA((2, n_seq)),
            pltpu.SemaphoreType.DMA((2, devices)),
            pltpu.SemaphoreType.DMA((2, devices)),
        ],
        compiler_params=pltpu.CompilerParams(
            collective_id=7, has_side_effects=True, vmem_limit_bytes=32 * MB
        ),
        name="reduce_weights",
    )(parts, small)


def rms_inverse(values):
    return lax.rsqrt(jnp.mean(values * values, axis=-1, keepdims=True) + eps)


def dot(a, b, dims, precision=None):
    return lax.dot_general(a, b, (dims, ((), ())), preferred_element_type=F32, precision=precision)


def local(
    n_head,
    n_seq,
    tokens,
    attn_gain,
    qkv_weight,
    bias_table,
    proj_weight,
    ffn_gain,
    router_weight,
    router_bias,
    expert_in,
    expert_out,
    bucket,
    expert_choice,
    priority,
    out_grad,
):
    tsd, seqs, width = tokens.shape
    buckets, heads_here = bias_table.shape
    head_dim = qkv_weight.shape[1] // (3 * heads_here)
    hidden = heads_here * head_dim
    length = bucket.shape[0] // 2
    own = out_grad.shape[1]
    ways = n_seq // seqs
    qlen = length // ways
    experts = router_weight.shape[1]
    devices = n_head * n_seq
    assert ways == 2 and n_head == 4 and own * n_head == seqs and experts == devices
    seq_index = lax.axis_index("seq")
    head_index = lax.axis_index("head")
    half = seq_index % ways

    share = tsd // n_head
    x_share = lax.dynamic_slice_in_dim(tokens, head_index * share, share, 0).astype(F32)
    n_share = (x_share * rms_inverse(x_share) * attn_gain).astype(BF16)
    normed1 = gather_rows(jnp.moveaxis(n_share, 1, 0), n_seq, ways, tsd)

    proj_full = lax.all_gather(proj_weight, "head", axis=0, tiled=True)

    reversed_bucket = jnp.concatenate([bucket[:1], bucket[:0:-1]])
    near = lax.dynamic_slice_in_dim(reversed_bucket, half * qlen, length + qlen, 0)
    onehot = (near[None, :] == jnp.arange(buckets, dtype=jnp.int32)[:, None]).astype(F32)
    window = dot(bias_table * LOG2E, onehot, ((0,), (0,)), HIGH)[:, None, :]

    qkv_t = dot(qkv_weight, normed1, ((0,), (1,))).astype(BF16)
    qkv_t = qkv_t.reshape(heads_here, 3, head_dim, length)
    query_t = lax.dynamic_slice_in_dim(qkv_t[:, 0], half * qlen, qlen, 2)
    attended_t, lse = attn_fwd(window, query_t, qkv_t, 1024, 1024)

    spread = to_residual(attended_t.reshape(hidden, qlen), own, ways, seqs, n_head, tsd)
    att_all = spread.reshape(own, n_head * hidden, tsd)
    branch = jnp.einsum("bcp,cd->bpd", att_all, proj_full, preferred_element_type=F32)
    rows = own * tsd
    x_own = lax.dynamic_slice_in_dim(tokens, head_index * own, own, 1).astype(F32)
    x_own = jnp.moveaxis(x_own, 1, 0).reshape(rows, width)
    inv1 = rms_inverse(x_own)
    mid = x_own + branch.reshape(rows, width)
    inv2 = rms_inverse(mid)
    normed2 = (mid * inv2 * ffn_gain).astype(BF16)
    logits = dot(normed2, router_weight, ((1,), (0,))) + router_bias
    gates = jax.nn.softmax(logits, axis=1)
    route = expert_choice.T.reshape(rows)
    order = priority.T.reshape(rows)
    same = (route[:, None] == route[None, :]) & (order[None, :] < order[:, None])
    rank = jnp.sum(same.astype(jnp.int32), axis=1)
    capacity = max(2, (5 * rows + 4 * experts - 1) // (4 * experts))
    slots = (capacity + 7) // 8 * 8
    keep = rank < capacity
    chosen = (route[:, None] == jnp.arange(experts, dtype=jnp.int32)[None, :]).astype(F32)
    gate = jnp.sum(gates * chosen, axis=1)
    upstream = jnp.moveaxis(out_grad, 1, 0).astype(F32).reshape(rows, width)
    grad_rows = (gate[:, None] * upstream).astype(BF16)
    slot = jnp.where(keep, route * (2 * slots) + rank, -1)
    slot = jnp.concatenate([slot, jnp.where(keep, slot + slots, -1)])
    placing = (slot[None, :] == jnp.arange(experts * 2 * slots, dtype=jnp.int32)[:, None]).astype(BF16)
    sending = dot(placing, jnp.concatenate([normed2, grad_rows], axis=0), ((1,), (0,))).astype(BF16)
    arriving = exchange(sending.reshape(devices, 2 * slots, width), n_head, n_seq, 4, "to_experts")

    arriving = arriving.reshape(devices, 2, slots, width)
    came = arriving[:, 0].reshape(devices * slots, width)
    came_grad = arriving[:, 1].reshape(devices * slots, width)
    pre = dot(came, expert_in[0], ((1,), (0,)))
    act_value, act_pull = jax.vjp(lambda v: jax.nn.gelu(v, approximate=True), pre)
    act = act_value.astype(BF16)
    result = dot(act, expert_out[0], ((1,), (0,))).astype(BF16)
    grad_act = dot(came_grad, expert_out[0], ((1,), (1,)))
    grad_pre = act_pull(grad_act)[0].astype(BF16)
    grad_slots = dot(grad_pre, expert_in[0], ((1,), (1,))).astype(BF16)
    grad_expert_out = dot(act, came_grad, ((0,), (0,)))[None]
    grad_expert_in = dot(came, grad_pre, ((0,), (0,)))[None]
    returning = jnp.stack(
        [result.reshape(devices, slots, width), grad_slots.reshape(devices, slots, width)], axis=1
    )
    back = exchange(returning.reshape(devices, 2 * slots, width), n_head, n_seq, 5, "from_experts")
    placed = dot(placing, back.reshape(devices * 2 * slots, width), ((0,), (0,)))
    expert_rows, grad_disp = placed[:rows], placed[rows:]

    output = mid + gate[:, None] * expert_rows
    output = jnp.moveaxis(output.astype(BF16).reshape(own, tsd, width), 0, 1)
    grad_gate = jnp.sum(upstream * expert_rows, axis=1)
    grad_logits = gates * (chosen - gate[:, None]) * grad_gate[:, None]
    grad_router_bias = jnp.sum(grad_logits, axis=0)
    grad_router_t = dot(grad_logits, normed2.astype(F32), ((0,), (0,)), HIGH)
    grad_normed2 = grad_disp + dot(grad_logits, router_weight.astype(F32), ((1,), (1,)), HIGH)
    scaled2 = grad_normed2 * ffn_gain
    unit2 = mid * inv2
    grad_ffn_gain = jnp.sum(grad_normed2 * unit2, axis=0)
    grad_mid = upstream + inv2 * (scaled2 - unit2 * jnp.mean(scaled2 * unit2, axis=-1, keepdims=True))
    grad_branch = grad_mid.astype(BF16).reshape(own, tsd, width)

    grad_att = jnp.einsum("cd,bpd->bcp", proj_full, grad_branch, preferred_element_type=F32)
    grad_att = grad_att.astype(BF16).reshape(own, n_head, hidden, tsd)
    grad_attended_t = to_attention(grad_att, own, ways, seqs, n_head, tsd)
    grad_proj = jnp.einsum("bcp,bpd->cd", att_all, grad_branch, preferred_element_type=F32)
    grad_proj = lax.psum_scatter(grad_proj.astype(BF16), "head", scatter_dimension=0, tiled=True)

    grad_q, grad_kv, grad_window = attn_bwd(
        window, query_t, qkv_t, attended_t, grad_attended_t.reshape(heads_here, head_dim, qlen), lse, 512, 1024
    )
    grad_table = dot(onehot, grad_window[:, 0], ((1,), (1,)), HIGH)
    wide_q = lax.dynamic_update_slice_in_dim(
        jnp.zeros((heads_here, head_dim, length), BF16), grad_q, half * qlen, 2
    )
    grad_qkv_t = jnp.concatenate([wide_q[:, None], grad_kv], axis=1).reshape(3 * hidden, length)
    grad_normed1 = dot(grad_qkv_t, qkv_weight, ((0,), (1,))).astype(BF16)
    grad_weight_t = dot(grad_qkv_t, normed1, ((1,), (0,)))
    grad_gain_part = jnp.sum(grad_weight_t * qkv_weight.T.astype(F32), axis=0)

    parts = jnp.concatenate([grad_weight_t.astype(BF16), grad_proj], axis=0)
    piece = -(-parts.shape[0] // (16 * n_seq)) * 16
    parts = jnp.pad(parts, ((0, piece * n_seq - parts.shape[0]), (0, 0)))
    table_whole = lax.dynamic_update_slice_in_dim(
        jnp.zeros((buckets, n_head * heads_here), F32), grad_table, head_index * heads_here, 1
    )
    extras = jnp.concatenate([grad_ffn_gain, grad_gain_part, grad_router_bias, table_whole.reshape(-1)])
    lanes = 128
    chunks = width // lanes
    extras = jnp.pad(extras, (0, devices * (8 - chunks) * lanes - extras.shape[0]))
    small = jnp.concatenate(
        [grad_router_t.reshape(experts, chunks, lanes), extras.reshape(devices, 8 - chunks, lanes)], axis=1
    )
    reduced, small = reduce_weights(parts.reshape(n_seq, piece, width), small, n_head, n_seq)
    reduced = reduced.reshape(n_seq * piece, width)
    grad_qkv_weight = reduced[: 3 * hidden].T.astype(F32)
    grad_proj_weight = reduced[3 * hidden : 3 * hidden + hidden].astype(F32)
    grad_router_weight = small[:, :chunks].reshape(experts, width).T
    extras = small[:, chunks:].reshape(-1)
    grad_ffn_gain = extras[:width]
    grad_attn_gain = extras[width : 2 * width] / attn_gain
    grad_router_bias = extras[2 * width : 2 * width + experts]
    table_whole = extras[2 * width + experts :][: buckets * n_head * heads_here]
    grad_bias_table = lax.dynamic_slice_in_dim(
        table_whole.reshape(buckets, n_head * heads_here), head_index * heads_here, heads_here, 1
    )

    grad_normed1_own = scatter_sums(grad_normed1, own, ways, n_seq, tsd).reshape(rows, width).astype(F32)
    unit1 = x_own * inv1
    scaled1 = grad_normed1_own * attn_gain
    grad_x = inv1 * (scaled1 - unit1 * jnp.mean(scaled1 * unit1, axis=-1, keepdims=True))
    grad_tokens = (grad_mid + grad_x).astype(BF16)
    grad_tokens = jnp.moveaxis(grad_tokens.reshape(own, tsd, width), 0, 1)
    return (
        output,
        grad_tokens,
        grad_attn_gain,
        grad_qkv_weight,
        grad_bias_table,
        grad_proj_weight,
        grad_ffn_gain,
        grad_router_weight,
        grad_router_bias,
        grad_expert_in,
        grad_expert_out,
    )


def solution(mesh):
    placed = (
        P("seq", None, None),
        P(),
        P(None, "head"),
        P(None, "head"),
        P("head", None),
        P(),
        P(),
        P(),
        P(("head", "seq"), None, None),
        P(("head", "seq"), None, None),
        P(),
        P("seq", "head"),
        P("seq", "head"),
        P("seq", "head", None),
    )
    return jax.shard_map(
        functools.partial(local, mesh.shape["head"], mesh.shape["seq"]),
        mesh=mesh,
        in_specs=placed,
        out_specs=(
            P("seq", "head", None),
            P("seq", "head", None),
            P(),
            P(None, "head"),
            P(None, "head"),
            P("head", None),
            P(),
            P(),
            P(),
            P(("head", "seq"), None, None),
            P(("head", "seq"), None, None),
        ),
        check_vma=False,
    )
```

time: 2670 us -> 685 us (0.26); the launches traced: 2630 us -> 679 us
  local copies, waits for them, and re-layouts: 1460 us -> 22.3 us
  Pallas kernels: 0 us -> 545 us
  matrix products: 445 us -> 82.4 us
  waiting for transfers between devices: 329 us -> 0.73 us
  other arithmetic: 295 us -> 14 us
  blocking collectives: 60.8 us -> 0 us
    unnamed x110 -> x77, local copies, waits for them, and re-layouts: 1210 us -> 7.23 us
    pallas_call x0 -> x9, Pallas kernels: none -> 545 us  [the longest x2 115 us: exchange(): pl.pallas_call(functools.partial(exchange_kernel, n_head, n_seq), out_sha...]
    dot_general x43 -> x19, matrix products: 445 us -> 82.4 us  [the longest x16 76.3 us: dot(): lax.dot_general(a, b, (dims, ((), ())), preferred_element_type=F32, preci...]
    reduce_scatter x3 -> x1, waiting for transfers between devices: 250 us -> 0.01 us  [local(): lax.psum_scatter(grad_proj.astype(BF16), 'head', scatter_dimension=0, til...]
    dynamic_update_slice x13 -> x0, other arithmetic: 158 us -> none  [the longest x12 158 us: local(): lax.map(attend_block, (group_query, group_keys, group_vals))]
    reduce_sum x9 -> x4, other arithmetic: 105 us -> 2.18 us  [the longest x1 1.26 us: local(): grad_gate = jnp.sum(upstream * expert_rows, axis=1)]
    reshape x14 -> x2, local copies, waits for them, and re-layouts: 87.1 us -> 0.2 us  [the longest x1 0.1 us: local(): table_whole.reshape(-1)]
    psum x2 -> x0, blocking collectives: 60.8 us -> none  [the longest x1 43.5 us: local(): lax.psum((grad_attn_gain, grad_ffn_gain, grad_router_weight, grad_router_...]
  transfers between devices with their start and end apart: 12 -> 2, of which waited for: 7 -> 0; matrix products, arithmetic and copies ran while one was open for 56% -> 6% of each run, Pallas kernels for 0% -> 33%
where the time goes in v1:
time: 685 us; the launch traced here: 679 us
  Pallas kernels  545 us (80%)
  matrix products  82.4 us (12%)
  local copies, waits for them, and re-layouts  22.3 us (3%)
  between operations  15 us (2%)
  other arithmetic  14 us (2%)
    pallas_call x2, Pallas kernels, exchange(): pl.pallas_call(functools.partial(exchange_kernel, n_head, n_seq), out_sha...  115 us
    pallas_call x1, Pallas kernels, attn_bwd(): pl.pallas_call(functools.partial(bwd_kernel, length, qlen, hd, bi, bj), g...  111 us
    dot_general x16, matrix products, dot(): lax.dot_general(a, b, (dims, ((), ())), preferred_element_type=F32, preci...  76.3 us
    pallas_call x1, Pallas kernels, scatter_sums(): pl.pallas_call(functools.partial(scatter_kernel, own, ways, groups), out_...  72.2 us
    pallas_call x1, Pallas kernels, reduce_weights(): pl.pallas_call(functools.partial(reduce_kernel, n_head, n_seq), out_shape...  69 us
    pallas_call x1, Pallas kernels, attn_fwd(): pl.pallas_call(functools.partial(fwd_kernel, length, qlen, hd, bi, bj), g...  57.3 us
    pallas_call x1, Pallas kernels, gather_rows(): pl.pallas_call(functools.partial(gather_kernel, n_seq, ways, tsd, piece),...  55.1 us
    pallas_call x1, Pallas kernels, to_residual(): pl.pallas_call(functools.partial(to_residual_kernel, own, ways, seqs, n_h...  36.5 us
  transfers between devices with their start and end apart: 2, of which 0 were waited for; matrix products, arithmetic and copies ran while one was open for 6% of the time, Pallas kernels for 33%

profile of v1, /device:TPU:12, one launch (start us, length us, event | category | flops | bytes accessed | tf_op | source)
XLA Modules:
  0.0 679.5 jit_solution(854269625492198362)
XLA Ops:
  10.7 55.1 %gather_rows.1 = bf16[4096,768]{1,0:T(8,128)(2,1)} custom-call(bf16[4,128,768]{2,1,0:T(8,128)(2,1)} %fusion.45.rows_in), custom_call_target="tpu_custom_call" | custom-call | tf_op jit(solution)/shard_map/gather_rows/pallas_call | solution.py:298
  65.8 9.0 %convolution_convert_fusion.1 = bf16[4096,576]{0,1:T(8,128)(2,1)} fusion(bf16[4096,768]{1,0:T(8,128)(2,1)} %gather_rows.1, bf16[768,576]{0,1:T(8,128)(2,1)} %param.16), kind=kOutput, calls=%fused_computation.14 | convolution fusion | flops 3626237952 | bytes 11894784 | tf_op jit(solution)/shard_map/dot_general | solution.py:646
  75.4 2.7 slice.74
  80.1 2.1 dynamic-slice_bitcast_fusion.q_ref
  82.2 57.3 %attn_forward.1 = (bf16[3,64,2048]{2,1,0:T(8,128)(2,1)}, f32[3,1,2048]{2,1,0:T(1,128)}) custom-call(f32[3,1,6144]{2,1,0:T(1,128)} %broadcast_in_dim.17.win_ref, bf16[3,64,2048]{2,1,0:T(8,128)(2,1)} %dynamic-slice_bitcast_fusion.q_ref, bf16[3,3,64,4096]{3,2,1,0:T(8,128)(2,1)} %bitcast.147, bf16[3,3,64,4096]{3,2,1,0:T(8,128)(2,1)} %bitcast.148), custom_call_target="tpu_custom_call" | custom-call | tf_op jit(solution)/shard_map/attn_forward/pallas_call | solution.py:77
  139.4 36.5 %to_residual.1 = bf16[1,4,192,512]{3,2,1,0:T(8,128)(2,1)} custom-call(bf16[192,2048]{1,0:T(8,128)(2,1)} %bitcast.161), custom_call_target="tpu_custom_call" | custom-call | tf_op jit(solution)/shard_map/to_residual/pallas_call | solution.py:360
  176.0 1.6 constant_dynamic-slice_fusion.2
  178.7 2.2 multiply_reduce_fusion.3
  183.0 4.0 fusion.17
  187.0 58.8 %to_experts.1 = bf16[32,48,768]{2,1,0:T(8,128)(2,1)} custom-call(bf16[32,48,768]{2,1,0:T(8,128)(2,1)} %bitcast.167), custom_call_target="tpu_custom_call" | custom-call | tf_op jit(solution)/shard_map/to_experts/pallas_call | solution.py:436
  245.8 1.9 fusion.72
  248.8 5.7 fusion.15
  254.6 6.2 fusion.40
  260.8 10.9 %fusion.6 = bf16[768,3072]{1,0:T(8,128)(2,1)S(1)} fusion(f32[768,3072]{1,0:T(8,128)} %copy-done.26, bf16[768,768]{1,0:T(8,128)(2,1)S(1)} %bitcast.169, bf16[1,3072,768]{2,1,0:T(8,128)(2,1)S(1)} %bitcast.188), kind=kOutput, calls=%fused_computation.8 | convolution fusion | flops 3671064576 | bytes 20054016 | tf_op jit(solution)/shard_map/dot_general | solution.py:646
  271.7 3.8 fusion.37
  275.5 1.7 pad_maximum_fusion.1
  277.2 56.1 %from_experts.1 = bf16[32,48,768]{2,1,0:T(8,128)(2,1)} custom-call(bf16[32,48,768]{2,1,0:T(8,128)(2,1)} %bitcast.152), custom_call_target="tpu_custom_call" | custom-call | tf_op jit(solution)/shard_map/from_experts/pallas_call | solution.py:436
  333.3 4.8 fusion.7
  339.6 1.3 multiply_reduce_fusion
  342.0 1.8 convolution_convert_fusion.2
  343.8 2.1 fusion.43
  347.0 29.6 %to_attention.1 = bf16[192,2048]{1,0:T(8,128)(2,1)} custom-call(bf16[1,4,192,512]{3,2,1,0:T(8,128)(2,1)} %bitcast.165), custom_call_target="tpu_custom_call" | custom-call | tf_op jit(solution)/shard_map/to_attention/pallas_call | solution.py:400
  376.7 110.5 %attn_backward.1 = (bf16[3,64,2048]{2,1,0:T(8,128)(2,1)}, bf16[3,2,64,4096]{3,2,1,0:T(8,128)(2,1)}, f32[3,1,6144]{2,1,0:T(1,128)}) custom-call(f32[3,1,6144]{2,1,0:T(1,128)} %broadcast_in_dim.17.win_ref, bf16[3,64,2048]{2,1,0:T(8,128)(2,1)} %dynamic-slice_bitcast_fusion.q_ref, bf16[3,3,64,4096]{3,2,1,0:T(8,128)(2,1)} %bitcast.149, ...), custom_call_target="tpu_custom_call" | custom-call | tf_op jit(solution)/shard_map/attn_backward/pallas_call | solution.py:163
  487.3 1.4 bitcast_dynamic-update-slice_fusion
  491.5 4.7 fusion.22
  496.2 7.0 %convolution_convert_fusion = bf16[4096,768]{1,0:T(8,128)(2,1)} fusion(bf16[576,4096]{1,0:T(8,128)(2,1)S(1)} %bitcast.158, bf16[768,576]{0,1:T(8,128)(2,1)S(1)} %copy-done.23), kind=kOutput, calls=%fused_computation.10 | convolution fusion | flops 3627024384 | bytes 11894784 | tf_op jit(solution)/shard_map/dot_general | solution.py:646
  505.6 72.2 %scatter_sums.1 = bf16[1,2,256,768]{3,2,1,0:T(8,128)(2,1)S(1)} custom-call(bf16[2,1,2,2,2,256,768]{6,5,4,3,2,1,0:T(8,128)(2,1)} %bitcast.156), custom_call_target="tpu_custom_call" | custom-call | tf_op jit(solution)/shard_map/scatter_sums/pallas_call | solution.py:538
  578.3 1.4 fusion.34
  579.7 9.1 %convolution_bitcast_fusion.1 = f32[1,768,3072]{2,1,0:T(8,128)} fusion(bf16[768,768]{1,0:T(8,128)(2,1)S(1)} %bitcast.160, bf16[768,3072]{1,0:T(8,128)(2,1)} %copy-done.6), kind=kOutput, calls=%fused_computation.16 | convolution fusion | flops 3623878656 | bytes 15335424 | tf_op jit(solution)/shard_map/dot_general | solution.py:646
  588.8 7.8 %convolution_bitcast_fusion = f32[1,3072,768]{2,1,0:T(8,128)} fusion(bf16[768,768]{1,0:T(8,128)(2,1)S(1)} %bitcast.170, f32[768,3072]{1,0:T(8,128)S(1)} %bitcast.192), kind=kOutput, calls=%fused_computation.15 | convolution fusion | flops 3645112320 | bytes 20054016 | tf_op jit(solution)/shard_map/dot_general | solution.py:646
  597.7 69.0 %reduce_weights.1 = (bf16[8,96,768]{2,1,0:T(8,128)(2,1)S(1)}, f32[32,8,128]{2,1,0:T(8,128)S(1)}) custom-call(bf16[8,96,768]{2,1,0:T(8,128)(2,1)S(1)} %bitcast.144, f32[32,8,128]{2,1,0:T(8,128)S(1)} %pad_maximum_fusion.3.small), custom_call_target="tpu_custom_call" | custom-call | tf_op jit(solution)/shard_map/reduce_weights/pallas_call | solution.py:616
  667.4 1.4 convert_bitcast_fusion
  (141 shorter events, 24.8 us)
Async XLA Ops:
  7.2 1.9 copy-start
  7.2 2.4 copy-start.19
  7.2 171.1 %all-gather.2.cloned.1.call-start = ((), (), s32[]{:S(2)}) async-start(), calls=%async_computation.1 | async-start | bytes 1474560 | tf_op jit(solution)/shard_map/all_gather | solution.py:687
  7.9 588.7 %reduce-scatter.2.cloned.1.call-start = ((), (), s32[]{:S(2)}) async-start(), calls=%async_computation.2 | async-start | bytes 1474560 | tf_op jit(solution)/shard_map/reduce_scatter | solution.py:764
  65.8 9.1 %copy-start.20 = (s32[8192]{0:T(1024)S(1)}, s32[8192]{0:T(1024)}, u32[]{:S(2)}) copy-start(s32[8192]{0:T(1024)} %param.24) | copy-start | bytes 98308
  74.8 4.2 copy-start.25
  175.9 2.0 copy-start.17
  176.0 2.0 copy-start.21
  177.9 3.1 copy-start.2
  178.7 2.2 copy-start.18
  181.0 1.3 copy-start.16
  181.0 1.8 copy-start.4
  245.8 8.7 %slice-start.2 = ((s8[4718592]{0:T(1024)(128)(4,1)}), s8[4194304]{0:T(1024)(128)(4,1)S(1)}, s32[]{:S(2)}) async-start(s8[4718592]{0:T(1024)(128)(4,1)} %bitcast.187), calls=%async_computation.5 | async-start | bytes 8388608
  247.8 13.0 %copy-start.13 = (bf16[32,1,24,768]{3,2,1,0:T(8,128)(2,1)}, bf16[32,1,24,768]{3,2,1,0:T(8,128)(2,1)S(1)}, u32[]{:S(2)}) copy-start(bf16[32,1,24,768]{3,2,1,0:T(8,128)(2,1)S(1)} %get-tuple-element.53) | copy-start | bytes 3538948
  248.8 5.8 slice-start.3
  254.5 6.2 copy-start.26
  254.6 17.1 %slice-start.4 = ((s8[4718592]{0:T(1024)(128)(4,1)}), s8[4194304]{0:T(1024)(128)(4,1)S(1)}, s32[]{:S(2)}) async-start(s8[4718592]{0:T(1024)(128)(4,1)} %bitcast.189), calls=%async_computation.7 | async-start | bytes 8388608
  260.8 10.9 %slice-start.5 = ((s8[4718592]{0:T(1024)(128)(4,1)}), s8[524288]{0:T(1024)(128)(4,1)S(1)}, s32[]{:S(2)}) async-start(s8[4718592]{0:T(1024)(128)(4,1)} %bitcast.189), calls=%async_computation.8 | async-start | bytes 1048576
  271.7 3.9 copy-start.6
  487.2 2.1 copy-start.12
  487.2 3.4 slice-start
  489.3 2.1 slice-start.1
  489.3 2.2 copy-start.23
  496.2 7.0 %copy-start.11 = (bf16[768,512]{0,1:T(8,128)(2,1)S(1)}, bf16[768,512]{0,1:T(8,128)(2,1)}, u32[]{:S(2)}) copy-start(bf16[768,512]{0,1:T(8,128)(2,1)} %fusion.96) | copy-start | bytes 2359300
  505.6 72.2 %copy-start.3 = (bf16[512,1,768]{2,0,1:T(8,128)(2,1)S(1)}, bf16[512,1,768]{2,0,1:T(8,128)(2,1)}, u32[]{:S(2)}) copy-start(bf16[512,1,768]{2,0,1:T(8,128)(2,1)} %copy-done.2) | copy-start | bytes 2359300
  505.6 83.2 %slice-start.6 = ((s8[9437184]{0:T(1024)(128)(4,1)}), s8[1048576]{0:T(1024)(128)(4,1)S(1)}, s32[]{:S(2)}) async-start(s8[9437184]{0:T(1024)(128)(4,1)} %bitcast.191), calls=%async_computation.9 | async-start | bytes 2097152
  578.3 1.4 copy-start.8
  578.3 10.5 %slice-start.7 = ((s8[9437184]{0:T(1024)(128)(4,1)}), s8[4194304]{0:T(1024)(128)(4,1)S(1)}, s32[]{:S(2)}) async-start(s8[9437184]{0:T(1024)(128)(4,1)} %bitcast.191), calls=%async_computation.10 | async-start | bytes 8388608
  579.7 9.1 %copy-start.14 = (bf16[32,1,24,768]{3,2,1,0:T(8,128)(2,1)S(1)}, bf16[32,1,24,768]{3,2,1,0:T(8,128)(2,1)}, u32[]{:S(2)}) copy-start(bf16[32,1,24,768]{3,2,1,0:T(8,128)(2,1)} %copy-done.13) | copy-start | bytes 3538948
  579.7 9.1 %slice-start.8 = ((s8[9437184]{0:T(1024)(128)(4,1)}), s8[4194304]{0:T(1024)(128)(4,1)S(1)}, s32[]{:S(2)}) async-start(s8[9437184]{0:T(1024)(128)(4,1)} %bitcast.191), calls=%async_computation.11 | async-start | bytes 8388608
  588.8 7.8 %copy-start.15 = (bf16[576,768]{1,0:T(8,128)(2,1)S(1)}, bf16[576,768]{1,0:T(8,128)(2,1)}, u32[]{:S(2)}) copy-start(bf16[576,768]{1,0:T(8,128)(2,1)} %get-tuple-element.56) | copy-start | bytes 2654212
  666.7 5.7 copy-start.1
  (6 other events, 7.0 us)
Sparse Core Ops, SparseCore 0:
  9.6 22.4 all-gather.1
  505.7 40.0 reduce-scatter.1

commit v2 on v0

v2 whole, which is shorter than its diff:
```python
import functools
import math

import jax
import jax.numpy as jnp
from jax import lax
from jax.experimental import pallas as pl
from jax.experimental.pallas import tpu as pltpu
from jax.sharding import PartitionSpec as P

F32 = jnp.float32
BF16 = jnp.bfloat16
LOG2E = math.log2(math.e)
MB = 1024 * 1024
eps = 1e-06
HIGH = lax.Precision.HIGHEST

def nt(a, b):
    return lax.dot_general(a, b, (((1,), (1,)), ((), ())), preferred_element_type=F32)


def nn(a, b):
    return jnp.dot(a, b, preferred_element_type=F32)


def biases(bucket, table):
    count = table.shape[1]
    row, column = (lax.broadcasted_iota(jnp.int32, (count, count), n) for n in (0, 1))
    table = jnp.sum(jnp.where(row == column, table, 0.0), axis=1, keepdims=True)
    same = bucket == lax.broadcasted_iota(jnp.int32, (count, bucket.shape[1]), 0)
    return jnp.sum(jnp.where(same, table * LOG2E, 0.0), axis=0, keepdims=True)


def turned(window):
    total = window.shape[1]
    base = pltpu.roll(jnp.broadcast_to(window, (8, total)), 0, 1, stride=1, stride_axis=0)
    return [pltpu.roll(base, 8 * a, 1) if a else base for a in range(16)]


def build_strip(window, strip):
    total = window.shape[1]
    for a, rows in enumerate(turned(window)):
        for d in range(total // 128 - 1):
            at = total - 128 - 128 * d
            strip[d * 128 + 8 * a : d * 128 + 8 * a + 8, :] = rows[:, at : at + 128]


def build_transposed(window, strip, wide):
    for a, rows in enumerate(turned(window)):
        wide[8 * a : 8 * a + 8, :] = rows
    for d in range(window.shape[1] // 128 - 1):
        strip[d * 128 : d * 128 + 128, :] = wide[:, 128 * d + 128 : 128 * d + 256].T


def fold_strip(strip, total):
    tiles = total // 128 - 1
    folded = jnp.zeros((8, total), F32)
    for a in range(16):
        pieces = [jnp.zeros((8, 128), F32)]
        for d in range(tiles - 1, -1, -1):
            pieces.append(strip[d * 128 + 8 * a : d * 128 + 8 * a + 8, :])
        wide = jnp.concatenate(pieces, axis=1)
        folded = folded + (pltpu.roll(wide, total - 8 * a, 1) if a else wide)
    at = lax.broadcasted_iota(jnp.int32, folded.shape, 0)
    for bit in (1, 2, 4):
        folded = jnp.where((at & bit) != 0, pltpu.roll(folded, total - bit, 1), folded)
    return jnp.sum(folded, axis=0, keepdims=True)


def three_rows(x):
    high = x.astype(BF16).astype(F32)
    mid = (x - high).astype(BF16).astype(F32)
    at = lax.broadcasted_iota(jnp.int32, (16, x.shape[1]), 0)
    rows = jnp.where(at == 0, high, jnp.where(at == 1, mid, jnp.where(at == 2, x - high - mid, 0.0)))
    return rows.astype(BF16)


def position(i, tsd, ways, half):
    return (i // tsd * ways + half) * tsd + i % tsd


def own_queries(q_ref, tsd, ways, half):
    blocks = q_ref.shape[3] // (tsd * ways)
    at = [pl.multiple_of((n * ways + half) * tsd, tsd) for n in range(blocks)]
    return jnp.concatenate([q_ref[0, 0, :, pl.ds(a, tsd)] for a in at], axis=1)


def forward_kernel(
    length, qlen, hd, tsd, bi, bj, half_ref, strip_ref, q_ref, k_ref, v_ref, out_ref, lse_ref, kaug, qaug, vaug
):
    ways = length // qlen
    half = half_ref[0]
    strip = strip_ref.at[0]
    scaled = own_queries(q_ref, tsd, ways, half).astype(F32) * (hd**-0.5 * LOG2E)
    high = scaled.astype(BF16)
    qaug[:hd, :] = high
    qaug[hd:, :] = (scaled - high.astype(F32)).astype(BF16)
    keys = k_ref[0, 0].T
    kaug[:, :hd] = keys
    kaug[:, hd:] = keys
    vaug[:hd, :] = v_ref[0, 0]
    vaug[hd:, :] = jnp.ones((16, length), BF16)

    def scores(i0, j0):
        raw = nn(kaug[pl.ds(j0, bj), :], qaug[:, pl.ds(i0, bi)])
        at = [j0 - position(i0 + 128 * c, tsd, ways, half) + length - 128 for c in range(bi // 128)]
        bias = [strip[pl.ds(pl.multiple_of(a, 128), bj), :] for a in at]
        return raw + jnp.concatenate(bias, axis=1)

    def store(i0, top, acc):
        total = acc[hd : hd + 1]
        out_ref[0, :, pl.ds(i0, bi)] = (acc[:hd] / total).astype(BF16)
        lse_ref[0, :, pl.ds(i0, bi)] = top + jnp.log2(total)
        return total

    def quick(ib, bounds):
        i0 = pl.multiple_of(ib * bi, bi)
        acc = jnp.zeros((hd + 16, bi), F32)
        for jb in range(length // bj):
            p = jnp.exp2(scores(i0, jb * bj)).astype(BF16)
            acc = acc + nn(vaug[:, jb * bj : (jb + 1) * bj], p)
        total = store(i0, 0.0, acc)
        return jnp.minimum(bounds[0], total), jnp.maximum(bounds[1], total)

    one = jnp.ones((1, bi), F32)
    low, high = lax.fori_loop(0, qlen // bi, quick, (one, one))
    fine = jnp.logical_and(jnp.min(low) > 2.0**-90, jnp.max(high) < 2.0**90)

    @pl.when(jnp.logical_not(fine))
    def _():
        def careful(ib, _):
            i0 = pl.multiple_of(ib * bi, bi)

            def step(jb, carry):
                top, acc = carry
                j0 = pl.multiple_of(jb * bj, bj)
                s = scores(i0, j0)
                new = jnp.maximum(top, jnp.max(s, axis=0, keepdims=True))
                p = jnp.exp2(s - new).astype(BF16)
                return new, acc * jnp.exp2(top - new) + nn(vaug[:, pl.ds(j0, bj)], p)

            start = (jnp.full((1, bi), -3e38, F32), jnp.zeros((hd + 16, bi), F32))
            store(i0, *lax.fori_loop(0, length // bj, step, start))
            return 0

        lax.fori_loop(0, qlen // bi, careful, 0)


def attend_forward(half, strips, qkv_t, qlen, tsd, bi=2048, bj=512):
    heads, _, hd, length = qkv_t.shape
    return pl.pallas_call(
        functools.partial(forward_kernel, length, qlen, hd, tsd, bi, bj),
        grid=(heads,),
        out_shape=[
            jax.ShapeDtypeStruct((heads, hd, qlen), BF16),
            jax.ShapeDtypeStruct((heads, 1, qlen), F32),
        ],
        in_specs=[
            pl.BlockSpec(memory_space=pltpu.SMEM),
            pl.BlockSpec((1,) + strips.shape[1:], lambda n: (n, 0, 0)),
            pl.BlockSpec((1, 1, hd, length), lambda n: (n, 0, 0, 0)),
            pl.BlockSpec((1, 1, hd, length), lambda n: (n, 1, 0, 0)),
            pl.BlockSpec((1, 1, hd, length), lambda n: (n, 2, 0, 0)),
        ],
        out_specs=[
            pl.BlockSpec((1, hd, qlen), lambda n: (n, 0, 0)),
            pl.BlockSpec((1, 1, qlen), lambda n: (n, 0, 0)),
        ],
        scratch_shapes=[
            pltpu.VMEM((length, 2 * hd), BF16),
            pltpu.VMEM((2 * hd, qlen), BF16),
            pltpu.VMEM((hd + 16, length), BF16),
        ],
        compiler_params=pltpu.CompilerParams(vmem_limit_bytes=56 * MB),
        cost_estimate=pl.CostEstimate(
            flops=4 * heads * hd * qlen * length,
            bytes_accessed=10 * heads * hd * length,
            transcendentals=heads * qlen * length,
        ),
        name="attend_forward",
    )(half, strips, qkv_t, qkv_t, qkv_t)


def sum_over_seq(head, seq, parts, got_y, sum_y, got_z, own_z, out, y_send, y_recv, z_send, z_recv):
    line, pair = lax.div(seq, 2), lax.rem(seq, 2)
    lines = parts.shape[0]
    beside = (head, seq ^ 1)
    far = [(k, (head, seq ^ (2 * k))) for k in range(1, lines)]
    mine = out.at[line, pair]

    def over_pair():
        return remote(parts.at[:, 1 - pair], got_y, y_send.at[0], y_recv.at[0], beside)

    def over_line(k, peer):
        return remote(sum_y.at[line ^ k], got_z.at[k], z_send.at[0, k], z_recv.at[0, k], peer)

    def back_line(k, peer):
        return remote(own_z, mine, z_send.at[1, k], z_recv.at[1, k], peer)

    def back_pair():
        return remote(own_z, mine, y_send.at[1], y_recv.at[1], beside)

    def pass_on(k):
        passed = out.at[line ^ k, pair]
        return remote(passed, passed, y_send.at[1 + k], y_recv.at[1 + k], beside)

    def first():
        over_pair().start()

    def second():
        over_pair().wait()
        for p in range(lines):
            sum_y[p] = (parts[p, pair].astype(F32) + got_y[p].astype(F32)).astype(BF16)
        for k, peer in far:
            over_line(k, peer).start()

    def third():
        total = sum_y[line].astype(F32)
        for k, peer in far:
            over_line(k, peer).wait()
            total = total + got_z[k].astype(F32)
        own_z[...] = total.astype(BF16)
        out[line, pair] = total.astype(BF16)
        for k, peer in far:
            back_line(k, peer).start()
        back_pair().start()

    def fourth():
        for k, peer in far:
            landed = out.at[line ^ k, pair]
            remote(landed, landed, z_send.at[1, k], z_recv.at[1, k], peer).wait_recv()
            pass_on(k).start()

    def fifth():
        for k, peer in far:
            back_line(k, peer).wait_send()
            pass_on(k).wait_send()
        back_pair().wait_send()
        for k in range(lines):
            landed = out.at[line ^ k, 1 - pair]
            remote(landed, landed, y_send.at[1 + k], y_recv.at[1 + k], beside).wait_recv()

    return first, second, third, fourth, fifth


def backward_kernel(
    length, qlen, hd, tsd, bi, bj, own, seqs, n_head, buckets,
    bucket_ref, strip_ref, q_ref, k_ref, v_ref, o_ref, lse_ref, w_ref, att, grad_branch, proj, normed,
    grad_ref, grad_table_ref, gain_ref, reduced, last,
    source, att_v, branch_v, weight_v, dstrip, kaug, qaug, vaug, daug, q_v, dk_acc, dv_acc, do_ref,
    rows_v, proj_v, got_p, pass_p, got_q, proj_sum, parts, got_y, sum_y, got_z, own_z, sums,
    send, recv, load_sem, p_send, p_recv, y_send, y_recv, z_send, z_recv,
):
    total = 2 * length
    ways = length // qlen
    head, seq = lax.axis_index("head"), lax.axis_index("seq")
    half = lax.rem(seq, ways)
    item = pl.program_id(0)
    heads = pl.num_programs(0)
    inner = line_to_batch(lax.div(seq, ways), seqs) % own
    mine = pl.multiple_of(lax.div(seq, ways) * tsd, tsd)

    def peer(k):
        number = lax.rem(lax.div(seq, ways) - k + seqs, seqs)
        to_head, to_inner = lax.div(number, own), lax.rem(number, own)
        to_seq = batch_to_line(head * own + to_inner, seqs) * ways + half
        return to_head, to_inner, to_seq, jnp.logical_and(to_head == head, to_seq == seq)

    def piece(k, n):
        to_head, to_inner, to_seq, is_self = peer(k)
        target = do_ref.at[n, :, pl.ds(mine, tsd)]
        return source.at[to_inner, to_head, n], target, send.at[k, n], recv.at[k, n], (to_head, to_seq), is_self

    sibling, cross = (head ^ 1, seq), (head ^ 2, seq)
    lines = parts.shape[1]
    others = [(head, seq ^ (2 * k)) for k in range(1, lines)] + [(head, seq ^ 1), sibling, cross]
    loads = [
        pltpu.make_async_copy(normed, rows_v, load_sem.at[0]),
        pltpu.make_async_copy(proj, weight_v, load_sem.at[1]),
        pltpu.make_async_copy(grad_branch, branch_v, load_sem.at[2]),
        pltpu.make_async_copy(att, att_v, load_sem.at[3]),
    ]
    hidden = proj_v.shape[1]

    @pl.when(item == 0)
    def _():
        for load in (loads[1], loads[2], loads[3], loads[0]):
            load.start()
        greet_both(own, ways, seqs, n_head, head, seq, others, wait=False)
        loads[1].wait()
        loads[2].wait()
        for b in range(own):
            grads = nt(weight_v[...], branch_v[b]).astype(BF16)
            for h in range(n_head):
                for n in range(source.shape[2]):
                    at = h * hidden + n * hd
                    source[b, h, n] = grads[at : at + hd]
        pl.semaphore_wait(pltpu.get_barrier_semaphore(), 2 * seqs + len(others))
        for k in range(seqs):
            start_any(*piece(k, 0))
        loads[3].wait()
        total = functools.reduce(jnp.add, [nn(att_v[b], branch_v[b]) for b in range(own)]).astype(BF16)
        for h in range(n_head):
            proj_v[h] = total[h * hidden : (h + 1) * hidden]
        for n, of in enumerate((1, 3)):
            remote(proj_v.at[head ^ of], got_p.at[n], p_send.at[n], p_recv.at[n], sibling).start()

    def proj_over_x():
        for n in range(2):
            remote(got_p.at[n], got_p.at[n], p_send.at[n], p_recv.at[n], sibling).wait()
        pass_p[...] = (proj_v[head ^ 2].astype(F32) + got_p[1].astype(F32)).astype(BF16)
        remote(pass_p, got_q, p_send.at[2], p_recv.at[2], cross).start()

    def proj_total():
        remote(pass_p, got_q, p_send.at[2], p_recv.at[2], cross).wait()
        total = proj_v[head].astype(F32) + got_p[0].astype(F32) + got_q[...].astype(F32)
        proj_sum[...] = total.astype(BF16)
        loads[0].wait()

    def stages(m):
        return sum_over_seq(
            head, seq, parts.at[m], got_y.at[m], sum_y.at[m], got_z.at[m], own_z.at[m], sums.at[m],
            y_send.at[m], y_recv.at[m], z_send.at[m], z_recv.at[m],
        )

    strip = strip_ref.at[0]
    scale = hd**-0.5
    q_v[...] = own_queries(q_ref, tsd, ways, half)
    scaled = q_v[...].astype(F32) * (scale * LOG2E)
    high = scaled.astype(BF16)
    rest = (scaled - high.astype(F32)).astype(BF16)
    blank = jnp.zeros((2 * hd - 16, qlen), BF16)
    qaug[...] = jnp.concatenate([high, rest, three_rows(-lse_ref[0]), blank], axis=0).T
    keys = k_ref[0, 0]
    kaug[:hd, :] = keys
    kaug[hd : 2 * hd, :] = keys
    kaug[2 * hd :, :] = jnp.ones((2 * hd, length), BF16)
    vaug[:hd, :] = v_ref[0, 0]
    vaug[hd:, :] = jnp.ones((hd, length), BF16)
    for k in range(seqs):
        j = lax.rem(head * own + inner + k, seqs)
        landed = do_ref.at[item, :, pl.ds(pl.multiple_of(j * tsd, tsd), tsd)]
        remote(landed, landed, send.at[k, item], recv.at[k, item], (head ^ 1, seq)).wait_recv()

    @pl.when(item < heads - 1)
    def _():
        for k in range(seqs):
            start_any(*piece(k, item + 1))

    do = do_ref[item]
    delta = jnp.sum(do.astype(F32) * o_ref[0].astype(F32), axis=0, keepdims=True)
    daug[...] = jnp.concatenate([do, three_rows(-delta), blank[: hd - 16]], axis=0).T
    dstrip[...] = jnp.zeros_like(dstrip)
    dk_acc[...] = jnp.zeros_like(dk_acc)
    dv_acc[...] = jnp.zeros_like(dv_acc)
    grad_ref[0, :hd, :] = jnp.zeros((hd, length), BF16)
    across = bj // 128
    run = min(bi, tsd)
    down = run // 128

    def rows(i, j0, count):
        return pl.ds(pl.multiple_of(i - j0 + length - 128, 128), count)

    before = stages(jnp.maximum(item - 1, 0))
    assert qlen // bi >= 4

    def step(ib, _):
        i0 = pl.multiple_of(ib * bi, bi)
        here = pl.ds(i0, bi)
        for n in (1, 2, 3):

            @pl.when(jnp.logical_and(item > 0, ib == n))
            def _():
                before[n]()

        @pl.when(jnp.logical_and(item == 0, ib == 1))
        def _():
            proj_over_x()

        places = [position(i0 + m * run, tsd, ways, half) for m in range(bi // run)]
        dq = jnp.zeros((hd, bi), F32)
        for jb in range(length // bj):
            j0 = jb * bj
            there = slice(j0, j0 + bj)
            s = nn(qaug[here, :], kaug[:, there])
            bias = [
                jnp.concatenate([strip[rows(i, j0 + 128 * c, run), :] for c in range(across)], axis=1)
                for i in places
            ]
            p = jnp.exp2(s + jnp.concatenate(bias, axis=0))
            ds = p * nn(daug[here, :], vaug[:, there])
            for m, i in enumerate(places):
                for g in range(1 - across, down):
                    parts = [
                        ds[m * run + a * 128 : m * run + (a + 1) * 128, (a - g) * 128 : (a - g + 1) * 128]
                        for a in range(down)
                        if 0 <= a - g < across
                    ]
                    dstrip[rows(i + 128 * g, j0, 128), :] += functools.reduce(jnp.add, parts)
            dsl = ds.astype(BF16)
            dv_acc[:, there] += nn(do_ref[item, :, here], p.astype(BF16))
            dk_acc[:, there] += nn(q_v[:, here], dsl)
            dq = dq + nt(k_ref[0, 0, :, there], dsl)
        dq = (dq * scale).astype(BF16)
        for m, i in enumerate(places):
            grad_ref[0, :hd, pl.ds(pl.multiple_of(i, run), run)] = dq[:, m * run : (m + 1) * run]
        return 0

    lax.fori_loop(0, qlen // bi, step, 0)
    grad_ref[0, hd : 2 * hd, :] = (dk_acc[...] * scale).astype(BF16)
    grad_ref[0, 2 * hd :, :] = dv_acc[...].astype(BF16)
    same = bucket_ref[...] == lax.broadcasted_iota(jnp.int32, (buckets, total), 0)
    table = jnp.sum(jnp.where(same, fold_strip(dstrip, total), 0.0), axis=1, keepdims=True)
    row, column = (lax.broadcasted_iota(jnp.int32, (buckets, 128), n) for n in (0, 1))
    table = jnp.sum(jnp.where(row == column, table, 0.0), axis=0, keepdims=True)
    grad_table_ref[0] = jnp.broadcast_to(table, grad_table_ref.shape[1:])

    @pl.when(item == 0)
    def _():
        proj_total()

    @pl.when(item > 0)
    def _():
        before[4]()

    count = 3 * hd
    grad_w = nn(grad_ref[0], rows_v[...])
    gain = jnp.sum(w_ref[...].astype(F32) * grad_w, axis=0, keepdims=True)
    gain_ref[0] = jnp.broadcast_to(gain, gain_ref.shape[1:])
    share = hidden // source.shape[2]
    whole = [grad_w.astype(BF16), proj_sum[pl.ds(pl.multiple_of(item * share, share), share), :]]
    size = parts.shape[3]
    if 2 * lines * size > count + share:
        whole.append(jnp.zeros((2 * lines * size - count - share, grad_w.shape[1]), BF16))
    whole = jnp.concatenate(whole, axis=0)
    for p in range(2 * lines):
        parts[item, p // 2, p % 2] = whole[p * size : (p + 1) * size]

    @pl.when(item < heads - 1)
    def _():
        stages(jnp.minimum(item, heads - 2))[0]()

    @pl.when(item == heads - 1)
    def _():
        stores = [
            pltpu.make_async_copy(sums, reduced, load_sem.at[0]),
            pltpu.make_async_copy(parts.at[parts.shape[0] - 1], last, load_sem.at[1]),
        ]
        for store in stores:
            store.start()
        for store in stores:
            store.wait()
        for n in range(source.shape[2]):
            for k in range(seqs):
                origin, target, sent, arrival, to, is_self = piece(k, n)

                @pl.when(jnp.logical_not(is_self))
                def _():
                    remote(origin, target, sent, arrival, to).wait_send()


def attend_backward(
    bucket, strips, qkv_t, out_t, lse, qkv_weight_t, att, grad_branch, proj, normed, buckets, n_head, n_seq, bi=512, bj=1024
):
    heads, hd, qlen = out_t.shape
    own, _, tsd = att.shape
    seqs = qlen // tsd
    length, width = normed.shape
    hidden = heads * hd
    total = 2 * length
    lines = n_seq // 2
    piece = -(-(3 * hd + hidden // heads) // (16 * n_seq)) * 16
    q_spec = pl.BlockSpec((1, hd, qlen), lambda n: (n, 0, 0))
    hbm = pl.BlockSpec(memory_space=pl.ANY)
    return pl.pallas_call(
        functools.partial(backward_kernel, length, qlen, hd, tsd, bi, bj, own, seqs, n_head, buckets),
        grid=(heads,),
        out_shape=[
            jax.ShapeDtypeStruct((heads, 3 * hd, length), BF16),
            jax.ShapeDtypeStruct((heads, 8, 128), F32),
            jax.ShapeDtypeStruct((heads, 8, width), F32),
            jax.ShapeDtypeStruct((heads - 1, lines, 2, piece, width), BF16),
            jax.ShapeDtypeStruct((lines, 2, piece, width), BF16),
        ],
        in_specs=[
            pl.BlockSpec((1, total), lambda n: (0, 0)),
            pl.BlockSpec((1,) + strips.shape[1:], lambda n: (n, 0, 0)),
            pl.BlockSpec((1, 1, hd, length), lambda n: (n, 0, 0, 0)),
            pl.BlockSpec((1, 1, hd, length), lambda n: (n, 1, 0, 0)),
            pl.BlockSpec((1, 1, hd, length), lambda n: (n, 2, 0, 0)),
            q_spec,
            pl.BlockSpec((1, 1, qlen), lambda n: (n, 0, 0)),
            pl.BlockSpec((3 * hd, width), lambda n: (n, 0)),
            hbm,
            hbm,
            hbm,
            hbm,
        ],
        out_specs=[
            pl.BlockSpec((1, 3 * hd, length), lambda n: (n, 0, 0)),
            pl.BlockSpec((1, 8, 128), lambda n: (n, 0, 0)),
            pl.BlockSpec((1, 8, width), lambda n: (n, 0, 0)),
            hbm,
            hbm,
        ],
        scratch_shapes=[
            pltpu.VMEM((own, n_head, heads, hd, tsd), BF16),
            pltpu.VMEM(att.shape, BF16),
            pltpu.VMEM(grad_branch.shape, BF16),
            pltpu.VMEM(proj.shape, BF16),
            pltpu.VMEM((total - 128, 128), F32),
            pltpu.VMEM((4 * hd, length), BF16),
            pltpu.VMEM((qlen, 4 * hd), BF16),
            pltpu.VMEM((2 * hd, length), BF16),
            pltpu.VMEM((qlen, 2 * hd), BF16),
            pltpu.VMEM((hd, qlen), BF16),
            pltpu.VMEM((hd, length), F32),
            pltpu.VMEM((hd, length), F32),
            pltpu.VMEM((heads, hd, qlen), BF16),
            pltpu.VMEM((length, width), BF16),
            pltpu.VMEM((n_head, hidden, width), BF16),
            pltpu.VMEM((2, hidden, width), BF16),
            pltpu.VMEM((hidden, width), BF16),
            pltpu.VMEM((hidden, width), BF16),
            pltpu.VMEM((hidden, width), BF16),
            pltpu.VMEM((heads, lines, 2, piece, width), BF16),
            pltpu.VMEM((heads - 1, lines, piece, width), BF16),
            pltpu.VMEM((heads - 1, lines, piece, width), BF16),
            pltpu.VMEM((heads - 1, lines, piece, width), BF16),
            pltpu.VMEM((heads - 1, piece, width), BF16),
            pltpu.VMEM((heads - 1, lines, 2, piece, width), BF16),
            pltpu.SemaphoreType.DMA((seqs, heads)),
            pltpu.SemaphoreType.DMA((seqs, heads)),
            pltpu.SemaphoreType.DMA((4,)),
            pltpu.SemaphoreType.DMA((3,)),
            pltpu.SemaphoreType.DMA((3,)),
            pltpu.SemaphoreType.DMA((heads - 1, 1 + lines)),
            pltpu.SemaphoreType.DMA((heads - 1, 1 + lines)),
            pltpu.SemaphoreType.DMA((heads - 1, 2, lines)),
            pltpu.SemaphoreType.DMA((heads - 1, 2, lines)),
        ],
        compiler_params=pltpu.CompilerParams(
            collective_id=3, has_side_effects=True, vmem_limit_bytes=62 * MB
        ),
        name="attend_backward",
    )(bucket, strips, qkv_t, qkv_t, qkv_t, out_t, lse, qkv_weight_t, att, grad_branch, proj, normed)


MESH = pl.DeviceIdType.MESH


def greet(peers, wait=True):
    barrier = pltpu.get_barrier_semaphore()
    for peer in peers:
        pl.semaphore_signal(barrier, inc=1, device_id=peer, device_id_type=MESH)
    if wait:
        pl.semaphore_wait(barrier, len(peers))


def remote(source, target, send, recv, peer):
    return pltpu.make_async_remote_copy(
        src_ref=source,
        dst_ref=target,
        send_sem=send,
        recv_sem=recv,
        device_id=peer,
        device_id_type=MESH,
    )


def start_any(source, target, send, recv, peer, is_self):
    @pl.when(is_self)
    def _():
        pltpu.make_async_copy(source, target, recv).start()

    @pl.when(jnp.logical_not(is_self))
    def _():
        remote(source, target, send, recv, peer).start()


def wait_any(source, target, send, recv, peer, is_self):
    remote(source, target, send, recv, peer).wait_recv()

    @pl.when(jnp.logical_not(is_self))
    def _():
        remote(source, target, send, recv, peer).wait_send()


def line_to_batch(line, seqs):
    return line % 2 * (seqs // 2) + line // 2


def batch_to_line(batch, seqs):
    return batch % (seqs // 2) * 2 + batch // (seqs // 2)


def gather_kernel(
    n_seq, ways, seqs, tsd, share, tokens, gain, w_ref, bucket, table, out, qkv_out, strips_f, strips_b,
    rows, qkv, tokens_v, rows_in, strip_v, wide, own_sem, a_send, a_recv, p_send, p_recv, o_sem, s_sem,
):
    head, seq = lax.axis_index("head"), lax.axis_index("seq")
    cross, sibling, beside = (head ^ 2, seq), (head ^ 1, seq), (head, seq ^ 1)
    lines = n_seq // 2
    first = pl.ds(pl.multiple_of(head * share, share), share)
    loads = [
        pltpu.make_async_copy(tokens.at[first], tokens_v.at[first], own_sem.at[0]),
        pltpu.make_async_copy(tokens, tokens_v, own_sem.at[1]),
    ]
    peers = [(head, seq ^ (2 * k)) for k in range(1, lines)] + [cross, sibling, beside]
    loads[0].start()
    greet(peers, wait=False)
    loads[0].wait()
    few = min(share, 64)

    gains = jnp.concatenate([gain[n : n + 1, :] for n in range(gain.shape[0])], axis=1)

    def normed(x):
        return (x * rms_inverse(x) * gains).astype(BF16)

    def part(t, _):
        x = tokens_v[pl.ds(head * share + t * few, few)].astype(F32)
        for n in range(seqs):
            rows_in[n, pl.ds(pl.multiple_of(t * few, few), few), :] = normed(x[:, n])
        return 0

    lax.fori_loop(0, share // few, part, 0)
    loads[1].start()
    pl.semaphore_wait(pltpu.get_barrier_semaphore(), len(peers))

    def share_of(k, of_head, part=None):
        at = (seq ^ k) * tsd + of_head * share
        if part is None:
            return rows.at[pl.ds(pl.multiple_of(at, share), share), :]
        return rows.at[pl.ds(pl.multiple_of(at + part * (share // 2), share // 2), share // 2), :]

    started = []

    def launch(source, target, send_sem, recv_sem, peer):
        copy = remote(source, target, send_sem, recv_sem, peer)
        copy.start()
        started.append(copy)

    def here(of_head):
        at = seq * tsd + of_head * share
        return rows.at[pl.ds(pl.multiple_of(at, share), share), :]

    queue = [k for k in range(1, lines) if k >= lines // 2] + [k for k in range(1, lines) if k < lines // 2]
    queue = queue[:1] + queue[lines // 2 :] + queue[1 : lines // 2]
    flying = []

    def dispatch():
        if queue:
            k = queue.pop(0)
            to = seq ^ (2 * k)
            source = rows_in.at[line_to_batch(lax.div(to, ways), seqs)]
            flying.append(remote(source, here(head), a_send.at[k], a_recv.at[k], (head, to)))
            flying[-1].start()

    order = list(queue)
    order = order[1:2] + order[:1] + order[2:]
    dispatch()
    dispatch()

    batch = line_to_batch(lax.div(seq, ways), seqs)
    loads[1].wait()

    def normalise(t, _):
        at = pl.ds(pl.multiple_of(t * few, few), few)
        all_here = tokens_v[at].astype(F32)
        x = all_here[:, 0]
        for n in range(1, seqs):
            x = jnp.where(batch == n, all_here[:, n], x)
        rows[pl.ds(pl.multiple_of(seq * tsd + t * few, few), few), :] = normed(x)
        return 0

    lax.fori_loop(0, tsd // few, normalise, 0)
    launch(here(head), here(head), p_send.at[1, 1], p_recv.at[1, 1], beside)

    heads = table.shape[0]
    jobs = [(n, kind) for n in range(heads) for kind in range(2)]
    strip_out = {}

    def build():
        if jobs:
            n, kind = jobs.pop(0)
            if kind in strip_out:
                strip_out[kind].wait()
            window = biases(bucket[...], table[n : n + 1, :])
            if kind == 0:
                build_transposed(window, strip_v.at[0], wide)
            else:
                build_strip(window, strip_v.at[1])
            target = (strips_f, strips_b)[kind].at[n]
            strip_out[kind] = pltpu.make_async_copy(strip_v.at[kind], target, s_sem.at[kind])
            strip_out[kind].start()

    def send(kind, k, of_head, peer, to_k=None, part=None):
        ref = share_of(k, of_head, part)
        to_k = k if to_k is None else to_k
        launch(ref, ref, p_send.at[kind, k], p_recv.at[kind, to_k], peer)

    def arrived(kind, k, of_head, part=None):
        ref = share_of(k, of_head, part)
        remote(ref, ref, p_send.at[kind, k], p_recv.at[kind, k], cross).wait_recv()

    def stage_own(k):
        if k:
            ref = share_of(2 * k, head)
            remote(ref, ref, a_send.at[k], a_recv.at[k], cross).wait_recv()
            send(0, 2 * k, head, cross)
            send(1, 2 * k, head, beside, 2 * k + 1)
            send(4, 2 * k, head, sibling)

    def stage_pass(k):
        if k:
            arrived(0, 2 * k, head ^ 2)
            send(2, 2 * k, head ^ 2, beside, 2 * k + 1, 0)
            send(5, 2 * k, head ^ 2, sibling)
        arrived(1, 2 * k + 1, head)
        send(3, 2 * k + 1, head, cross, None, 1 if k else None)
        send(6, 2 * k + 1, head, sibling)

    def stage_last(k):
        if k:
            arrived(2, 2 * k + 1, head ^ 2, 0)
            arrived(3, 2 * k + 1, head ^ 2, 1)
        else:
            arrived(3, 1, head ^ 2)
        send(7, 2 * k + 1, head ^ 2, sibling)

    def project(k, even):
        block = 2 * k + (0 if even else 1)
        if even and block:
            arrived(4, block, head ^ 1)
            arrived(5, block, head ^ 3)
        elif block:
            arrived(6, block, head ^ 1)
            arrived(7, block, head ^ 3)
        at = pl.ds(pl.multiple_of((seq ^ block) * tsd, tsd), tsd)
        qkv[:, at] = nt(w_ref[...], rows[at, :]).astype(BF16)
        for n, (source, target) in enumerate(((rows.at[at, :], out.at[at, :]), (qkv.at[:, at], qkv_out.at[:, at]))):
            copy = pltpu.make_async_copy(source, target, o_sem.at[n, block])
            copy.start()
            stored.append(copy)

    stored = []
    project(0, True)
    build()
    order = [0] + order
    for step in range(len(order) + 2):
        if step < len(order):
            stage_own(order[step])
            if step and queue:
                flying.pop(0).wait_send()
                dispatch()
        if 0 <= step - 1 < len(order):
            stage_pass(order[step - 1])
        if 0 <= step - 2 < len(order):
            stage_last(order[step - 2])
            if order[step - 2]:
                project(order[step - 2], True)
        if 0 <= step - 3 < len(order):
            project(order[step - 3], False)
        build()
    project(order[-1], False)
    for copy in started + flying:
        copy.wait_send()
    while jobs:
        build()
    for copy in stored + list(strip_out.values()):
        copy.wait()


def gather_rows(tokens, gain, qkv_weight_t, bucket, table, n_head, n_seq, ways):
    tsd, seqs, width = tokens.shape
    share = tsd // n_head
    length = n_seq * tsd
    columns = qkv_weight_t.shape[0]
    strips = (table.shape[0], 2 * length - 128, 128)
    hbm = pl.BlockSpec(memory_space=pl.ANY)
    vmem = pl.BlockSpec(memory_space=pltpu.VMEM)
    return pl.pallas_call(
        functools.partial(gather_kernel, n_seq, ways, seqs, tsd, share),
        out_shape=[
            jax.ShapeDtypeStruct((length, width), BF16),
            jax.ShapeDtypeStruct((columns, length), BF16),
            jax.ShapeDtypeStruct(strips, F32),
            jax.ShapeDtypeStruct(strips, F32),
        ],
        in_specs=[hbm, vmem, vmem, vmem, vmem],
        out_specs=[hbm] * 4,
        scratch_shapes=[
            pltpu.VMEM((length, width), BF16),
            pltpu.VMEM((columns, length), BF16),
            pltpu.VMEM(tokens.shape, BF16),
            pltpu.VMEM((seqs, share, width), BF16),
            pltpu.VMEM((2,) + strips[1:], F32),
            pltpu.VMEM((128, 2 * length), F32),
            pltpu.SemaphoreType.DMA((2,)),
            pltpu.SemaphoreType.DMA((n_seq // 2,)),
            pltpu.SemaphoreType.DMA((n_seq // 2,)),
            pltpu.SemaphoreType.DMA((8, n_seq)),
            pltpu.SemaphoreType.DMA((8, n_seq)),
            pltpu.SemaphoreType.DMA((2, n_seq)),
            pltpu.SemaphoreType.DMA((2,)),
        ],
        compiler_params=pltpu.CompilerParams(
            collective_id=1, has_side_effects=True, vmem_limit_bytes=60 * MB
        ),
        name="gather_rows",
    )(tokens, gain, qkv_weight_t, bucket, table)


def to_residual_kernel(own, ways, seqs, n_head, tsd, source, proj, out, proj_out, send, recv, p_sem, p_send, p_recv):
    head, seq = lax.axis_index("head"), lax.axis_index("seq")
    batch, half = line_to_batch(lax.div(seq, ways), seqs), lax.rem(seq, ways)
    to_head = lax.div(batch, own)
    inner = lax.rem(batch, own)
    mine_half = lax.rem(seq, ways)
    mine_at = lax.div(seq, ways)
    sibling, cross = (head ^ 1, seq), (head ^ 2, seq)
    greet_both(own, ways, seqs, n_head, head, seq, (sibling, cross))
    kept = pltpu.make_async_copy(proj, proj_out.at[head], p_sem)
    kept.start()
    moves = [
        remote(proj, proj_out.at[head], p_send.at[0], p_recv.at[0], cross),
        remote(proj, proj_out.at[head], p_send.at[1], p_recv.at[1], sibling),
    ]
    for move in moves:
        move.start()
    calls = []
    for k in range(seqs):
        j = lax.rem(head * own + inner + k, seqs)
        to_seq = j * ways + half
        is_self = jnp.logical_and(to_head == head, to_seq == seq)
        piece = source.at[:, pl.ds(pl.multiple_of(j * tsd, tsd), tsd)]
        args = (piece, out.at[inner, head], send.at[k], recv.at[k], (to_head, to_seq), is_self)
        start_any(*args)
        calls.append(args)
    passed = proj_out.at[head ^ 2]
    remote(passed, passed, p_send.at[0], p_recv.at[0], cross).wait_recv()
    moves.append(remote(passed, passed, p_send.at[2], p_recv.at[2], sibling))
    moves[2].start()
    for n, of in ((1, head ^ 1), (2, head ^ 3)):
        landed = proj_out.at[of]
        remote(landed, landed, p_send.at[n], p_recv.at[n], sibling).wait_recv()
    for move in moves:
        move.wait_send()
    kept.wait()
    for k, args in enumerate(calls):
        number = lax.rem(mine_at - k + seqs, seqs)
        from_head, from_inner = lax.div(number, own), lax.rem(number, own)
        landed = out.at[from_inner, from_head]
        remote(landed, landed, send.at[k], recv.at[k], (to_head, seq)).wait_recv()
        piece, target, sem, arrival, peer, is_self = args

        @pl.when(jnp.logical_not(is_self))
        def _():
            remote(piece, target, sem, arrival, peer).wait_send()


def greet_both(own, ways, seqs, n_head, head, seq, others=(), wait=True):
    batch, half = line_to_batch(lax.div(seq, ways), seqs), lax.rem(seq, ways)
    inner = lax.rem(batch, own)
    mine_half, mine_at = lax.rem(seq, ways), lax.div(seq, ways)
    barrier = pltpu.get_barrier_semaphore()
    for k in range(seqs):
        j = lax.rem(head * own + inner + k, seqs)
        number = lax.rem(mine_at - k + seqs, seqs)
        source_seq = batch_to_line(head * own + lax.rem(number, own), seqs) * ways + mine_half
        for peer in ((lax.div(batch, own), j * ways + half), (lax.div(number, own), source_seq)):
            pl.semaphore_signal(barrier, inc=1, device_id=peer, device_id_type=MESH)
    for peer in others:
        pl.semaphore_signal(barrier, inc=1, device_id=peer, device_id_type=MESH)
    if wait:
        pl.semaphore_wait(barrier, 2 * seqs + len(others))


def to_residual(source, proj, own, ways, seqs, n_head, tsd):
    rows = source.shape[0]
    hbm = pl.BlockSpec(memory_space=pl.ANY)
    return pl.pallas_call(
        functools.partial(to_residual_kernel, own, ways, seqs, n_head, tsd),
        out_shape=[
            jax.ShapeDtypeStruct((own, n_head, rows, tsd), BF16),
            jax.ShapeDtypeStruct((n_head,) + proj.shape, BF16),
        ],
        in_specs=[hbm, hbm],
        out_specs=[hbm, hbm],
        scratch_shapes=[
            pltpu.SemaphoreType.DMA((seqs,)),
            pltpu.SemaphoreType.DMA((seqs,)),
            pltpu.SemaphoreType.DMA,
            pltpu.SemaphoreType.DMA((3,)),
            pltpu.SemaphoreType.DMA((3,)),
        ],
        compiler_params=pltpu.CompilerParams(collective_id=2, has_side_effects=True),
        name="to_residual",
    )(source, proj)


SQRT_2_PI = math.sqrt(2.0 / math.pi)


def tn(a, b):
    return lax.dot_general(a, b, (((0,), (0,)), ((), ())), preferred_element_type=F32)


def experts_kernel(
    n_head, n_seq, mains, tails, tile,
    sending, w_in, w_out, back, rows_out, grads_out, act_out, pre_out,
    got, ret, v_in, v_out, rows_all, grads_all, act_all, pre_all,
    send, recv, r_send, r_recv, w_sem, o_sem,
):
    width, hidden = v_in.shape
    devices = n_head * n_seq
    me = lax.axis_index("head") * n_seq + lax.axis_index("seq")
    group = 8
    count = group * (16 * mains + 8 * tails)
    fold = width // 2
    base = mains * 2 * width

    def place(k):
        other = me ^ k
        return lax.div(other, n_seq), lax.rem(other, n_seq)

    barrier = pltpu.get_barrier_semaphore()

    def signal(k, _):
        pl.semaphore_signal(barrier, inc=1, device_id=place(k), device_id_type=MESH)
        return 0

    lax.fori_loop(1, devices, signal, 0)
    load_in = pltpu.make_async_copy(w_in, v_in, w_sem.at[0])
    load_out = pltpu.make_async_copy(w_out, v_out, w_sem.at[1])
    load_in.start()
    load_out.start()
    pl.semaphore_wait(barrier, devices - 1)
    mine = pltpu.make_async_copy(sending.at[me], got.at[me], recv.at[0])
    mine.start()

    def dispatch(k, _):
        remote(sending.at[me ^ k], got.at[me], send.at[k], recv.at[k], place(k)).start()
        return 0

    lax.fori_loop(1, devices, dispatch, 0)
    load_in.wait()
    load_out.wait()
    low = lax.broadcasted_iota(jnp.int32, (8, width), 0) < 4

    def chunk(c, _):
        first = c * count

        @pl.when(c == 0)
        def _():
            mine.wait()

        for i in range(group):
            k = c * group + i

            @pl.when(k > 0)
            def _():
                landed = got.at[me ^ k]
                remote(landed, landed, send.at[k], recv.at[k], place(k)).wait_recv()

        for i in range(group):
            source = me ^ (c * group + i)
            for j in range(mains):
                at = pl.ds(pl.multiple_of(first + (j * group + i) * 16, 16), 16)
                rows_all[at, :] = got[source, :, j * 2 * width : j * 2 * width + width]
                grads_all[at, :] = got[source, :, j * 2 * width + width : (j + 1) * 2 * width]
        for u in range(tails):
            for i in range(0, group, 2):
                rows, grads = [], []
                for n in range(2):
                    folded = got[me ^ (c * group + i + n), :, base + u * fold : base + (u + 1) * fold].astype(F32)
                    wide = jnp.concatenate([folded[:8], folded[8:]], axis=1)
                    rows.append(jnp.where(low, wide, 0.0))
                    grads.append(jnp.where(low, pltpu.roll(wide, 4, 0), 0.0))
                at = pl.ds(pl.multiple_of(first + mains * group * 16 + u * group * 8 + i * 8, 16), 16)
                rows_all[at, :] = jnp.concatenate(rows, axis=0).astype(BF16)
                grads_all[at, :] = jnp.concatenate(grads, axis=0).astype(BF16)
        here = pl.ds(pl.multiple_of(first, 16), count)
        x, d = rows_all[here, :], grads_all[here, :]

        def slab(t, carry):
            result, slots = carry
            columns = pl.ds(pl.multiple_of(t * tile, tile), tile)
            pre = nn(x, v_in[:, columns])
            square = pre * pre
            t_value = jnp.tanh(SQRT_2_PI * pre * (1.0 + 0.044715 * square))
            cdf = 0.5 * (1.0 + t_value)
            act = (pre * cdf).astype(BF16)
            slope = cdf + 0.5 * pre * (1.0 - t_value * t_value) * (SQRT_2_PI * (1.0 + 0.134145 * square))
            grad_pre = (nt(d, v_out[columns, :]) * slope).astype(BF16)
            act_all[here, columns] = act
            pre_all[here, columns] = grad_pre
            return result + nn(act, v_out[columns, :]), slots + nt(grad_pre, v_in[:, columns])

        zero = jnp.zeros((count, width), F32)
        result, slots = lax.fori_loop(0, hidden // tile, slab, (zero, zero))
        for i in range(group):
            source = me ^ (c * group + i)
            for j in range(mains):
                at = (j * group + i) * 16
                ret[source, :, j * 2 * width : j * 2 * width + width] = result[at : at + 16].astype(BF16)
                ret[source, :, j * 2 * width + width : (j + 1) * 2 * width] = slots[at : at + 16].astype(BF16)
            for u in range(tails):
                at = mains * group * 16 + u * group * 8 + i * 8
                wide = jnp.where(low, result[at : at + 8], pltpu.roll(slots[at : at + 8], 4, 0))
                folded = jnp.concatenate([wide[:, :fold], wide[:, fold:]], axis=0)
                ret[source, :, base + u * fold : base + (u + 1) * fold] = folded.astype(BF16)
        for i in range(group):
            k = c * group + i

            @pl.when(k == 0)
            def _():
                pltpu.make_async_copy(ret.at[me], back.at[me], r_recv.at[0]).start()

            @pl.when(k > 0)
            def _():
                remote(ret.at[me ^ k], back.at[me], r_send.at[k], r_recv.at[k], place(k)).start()

        return 0

    lax.fori_loop(0, devices // group, chunk, 0)

    kept = []
    for n, (source, target) in enumerate(
        ((rows_all, rows_out), (grads_all, grads_out), (act_all, act_out), (pre_all, pre_out))
    ):
        copy = pltpu.make_async_copy(source, target, o_sem.at[n])
        copy.start()
        kept.append(copy)
    for copy in kept:
        copy.wait()
    pltpu.make_async_copy(ret.at[me], back.at[me], r_recv.at[0]).wait()

    def finish(k, _):
        landed = back.at[me ^ k]
        remote(landed, landed, r_send.at[k], r_recv.at[k], place(k)).wait()
        remote(landed, landed, send.at[k], recv.at[k], place(k)).wait_send()
        return 0

    lax.fori_loop(1, devices, finish, 0)


def run_experts(sending, expert_in, expert_out, n_head, n_seq, mains, tails):
    devices = n_head * n_seq
    width, hidden = expert_in.shape
    rows = devices * (16 * mains + 8 * tails)
    tile = width
    hbm = pl.BlockSpec(memory_space=pl.ANY)
    return pl.pallas_call(
        functools.partial(experts_kernel, n_head, n_seq, mains, tails, tile),
        out_shape=[
            jax.ShapeDtypeStruct(sending.shape, BF16),
            jax.ShapeDtypeStruct((rows, width), BF16),
            jax.ShapeDtypeStruct((rows, width), BF16),
            jax.ShapeDtypeStruct((rows, hidden), BF16),
            jax.ShapeDtypeStruct((rows, hidden), BF16),
        ],
        in_specs=[hbm] * 3,
        out_specs=[hbm] * 5,
        scratch_shapes=[
            pltpu.VMEM(sending.shape, BF16),
            pltpu.VMEM(sending.shape, BF16),
            pltpu.VMEM((width, hidden), BF16),
            pltpu.VMEM((hidden, width), BF16),
            pltpu.VMEM((rows, width), BF16),
            pltpu.VMEM((rows, width), BF16),
            pltpu.VMEM((rows, hidden), BF16),
            pltpu.VMEM((rows, hidden), BF16),
            pltpu.SemaphoreType.DMA((devices,)),
            pltpu.SemaphoreType.DMA((devices,)),
            pltpu.SemaphoreType.DMA((devices,)),
            pltpu.SemaphoreType.DMA((devices,)),
            pltpu.SemaphoreType.DMA((2,)),
            pltpu.SemaphoreType.DMA((4,)),
        ],
        compiler_params=pltpu.CompilerParams(
            collective_id=4, has_side_effects=True, vmem_limit_bytes=60 * MB
        ),
        name="run_experts",
    )(sending, expert_in, expert_out)


def weights_kernel(rows_ref, grads_ref, act_ref, pre_ref, g_in_ref, g_out_ref):
    g_out_ref[...] = tn(act_ref[...], grads_ref[...])
    g_in_ref[...] = tn(rows_ref[...], pre_ref[...])


def expert_weights(rows, grads, act, pre):
    count, width = rows.shape
    hidden = act.shape[1]
    tile = width
    whole = pl.BlockSpec((count, width), lambda t: (0, 0))
    column = pl.BlockSpec((count, tile), lambda t: (0, t))
    return pl.pallas_call(
        weights_kernel,
        grid=(hidden // tile,),
        out_shape=[jax.ShapeDtypeStruct((width, hidden), F32), jax.ShapeDtypeStruct((hidden, width), F32)],
        in_specs=[whole, whole, column, column],
        out_specs=[pl.BlockSpec((width, tile), lambda t: (0, t)), pl.BlockSpec((tile, width), lambda t: (t, 0))],
        compiler_params=pltpu.CompilerParams(vmem_limit_bytes=48 * MB),
        cost_estimate=pl.CostEstimate(
            flops=4 * count * width * hidden, bytes_accessed=12 * width * hidden, transcendentals=0
        ),
        name="expert_weights",
    )(rows, grads, act, pre)


def finish_kernel(
    n_head, n_seq, ways, groups,
    buckets, grads, w_ref, weights, small_ref, gains, tables, out, weights_out, small_out,
    small, sent1, mine, got1, got2, got3, sum1, sum2, got_w, sum_w, got_z, own_w, got_near, sum_near, got_far, own_small, all_small,
    send, recv, y_send, y_recv, z_send, z_recv, near_sends, near_recvs, far_sends, far_recvs,
):
    head, seq = lax.axis_index("head"), lax.axis_index("seq")
    core, x = lax.rem(head, 2), lax.div(head, 2)
    y = lax.rem(seq, ways)
    sibling, cross, beside = (head ^ 1, seq), (head ^ 2, seq), (head, seq ^ 1)
    line, lines = lax.div(seq, 2), n_seq // 2
    side = x ^ lax.rem(lax.div(line, 2), 2)
    length = grads.shape[1]
    tsd = length // n_seq
    rows = tsd // 2

    near = [(head ^ (k // 2), seq ^ (k % 2)) for k in range(1, 2 * n_head)]
    far = [(head, seq ^ (2 * k)) for k in range(1, lines)]
    greet(near + far, wait=False)
    small[...] = small_ref[...]
    width = w_ref.shape[1]
    chunks = width // 128
    extra = 8 - chunks
    gain = functools.reduce(jnp.add, [gains[n, :1, :] for n in range(gains.shape[0])])
    for n in range(chunks):
        tile, row = (chunks + n) // extra, chunks + (chunks + n) % extra
        small[tile // n_seq, tile % n_seq // 2, tile % 2, row : row + 1, :] = gain[:, n * 128 : (n + 1) * 128]
    rows_of = [tables[n, :1, :buckets] for n in range(tables.shape[0])]
    rows_of.append(jnp.zeros((1, 128 - buckets * len(rows_of)), F32))
    tile = 8 + head
    small[lax.div(tile, n_seq), lax.div(lax.rem(tile, n_seq), 2), lax.rem(tile, 2), chunks : chunks + 1, :] = (
        jnp.concatenate(rows_of, axis=1)
    )
    waits = []

    def go(source, target, send_sem, recv_sem, peer):
        copy = remote(source, target, send_sem, recv_sem, peer)
        copy.start()
        waits.append(copy)

    def landed(target, send_sem, recv_sem, peer=sibling):
        remote(target, target, send_sem, recv_sem, peer).wait_recv()

    first, second_w, third, fourth, fifth = sum_over_seq(
        head, seq, weights, got_w, sum_w, got_z, own_w, weights_out, y_send, y_recv, z_send, z_recv
    )
    order = [(1, 1), (1, 0), (0, 1), (0, 0)]

    def grad_rows(of_core, v, dx, dy):
        block = of_core * 4 * groups + v * 4 + (side ^ dx) * 2 + (y ^ dy)
        at = pl.ds(pl.multiple_of(block * tsd, tsd), tsd)
        return tn(grads[:, at], w_ref[...])

    def pass_on(v, b):
        dx, dy = order[b]
        landed(got1.at[v, b], send.at[0, v, b], recv.at[0, v, b])
        total = (mine[v, b] + got1[v, b].astype(F32)).astype(BF16)
        sum1[v, b, 0] = total[:rows]
        sum1[v, b, 1] = total[rows:]
        if dx == 1:
            to = 1 - dy
            go(sum1.at[v, b, 0], got2.at[v, to], send.at[1, v, to], recv.at[1, v, to], cross)
        if dy == 1:
            to = 3 - dx
            go(sum1.at[v, b, 1], got2.at[v, to], send.at[1, v, to], recv.at[1, v, to], beside)

    pair = lax.rem(seq, 2)
    before = None
    for v in range(groups):
        for b, (dx, dy) in enumerate(order):
            sent1[v, b] = grad_rows(1 - core, v, dx, dy).astype(BF16)
            if before is None:
                pl.semaphore_wait(pltpu.get_barrier_semaphore(), len(near) + len(far))
                for k, peer in enumerate(near, 1):
                    part = small.at[head ^ (k // 2), :, pair ^ (k % 2)]
                    go(part, got_near.at[k], near_sends.at[0, k], near_recvs.at[0, k], peer)
            go(sent1.at[v, b], got1.at[v, b], send.at[0, v, b], recv.at[0, v, b], sibling)
            mine[v, b] = grad_rows(core, v, dx, dy)
            if before is None:
                first()
            if before is not None:
                pass_on(*before)
            before = (v, b)
    pass_on(*before)

    kept = {
        0: (order.index((0, 1)), 0),
        1: (order.index((0, 0)), 0),
        2: (order.index((1, 0)), 1),
        3: (order.index((0, 0)), 1),
    }

    def second(v, slot):
        landed(got2.at[v, slot], send.at[1, v, slot], recv.at[1, v, slot])
        b, w = kept[slot]
        sum2[v, slot] = (sum1[v, b, w].astype(F32) + got2[v, slot].astype(F32)).astype(BF16)
        if slot == 0:
            go(sum2.at[v, 0], got3.at[v, 0], send.at[2, v, 0], recv.at[2, v, 0], beside)
        if slot == 2:
            go(sum2.at[v, 2], got3.at[v, 1], send.at[2, v, 1], recv.at[2, v, 1], cross)

    total = small[head, :, pair]
    for k in range(1, 2 * n_head):
        landed(got_near.at[k], near_sends.at[0, k], near_recvs.at[0, k])
        total = total + got_near[k]
    sum_near[...] = total
    for k, peer in enumerate(far, 1):
        go(sum_near.at[line ^ k], got_far.at[k], far_sends.at[0, k], far_recvs.at[0, k], peer)
    second_w()
    total = sum_near[line]
    for k in range(1, lines):
        landed(got_far.at[k], far_sends.at[0, k], far_recvs.at[0, k])
        total = total + got_far[k]
    own_small[...] = total
    all_small[line] = total
    for k, peer in enumerate(far, 1):
        go(own_small, all_small.at[line], far_sends.at[1, k], far_recvs.at[1, k], peer)
    for v in range(groups):
        second(v, 0)
    for k in range(1, lines):
        landed(all_small.at[line ^ k], far_sends.at[1, k], far_recvs.at[1, k])
    small_out[head, :, pair] = all_small[...]
    for k, peer in enumerate(near, 1):
        go(all_small, small_out.at[head, :, pair], near_sends.at[1, k], near_recvs.at[1, k], peer)
    for v in range(groups):
        second(v, 2)
    third()
    for slot in (1, 3):
        for v in range(groups):
            second(v, slot)
    fourth()
    for w in (1, 0):
        for v in range(groups):
            landed(got3.at[v, w], send.at[2, v, w], recv.at[2, v, w])
            out[v, w] = (sum2[v, 1 + 2 * w].astype(F32) + got3[v, w].astype(F32)).astype(BF16)
    for k in range(1, 2 * n_head):
        part = small_out.at[head ^ (k // 2), :, pair ^ (k % 2)]
        landed(part, near_sends.at[1, k], near_recvs.at[1, k])
    fifth()
    for copy in waits:
        copy.wait_send()


def finish_sums(grads, qkv_weight_t, weights, small, gains, tables, buckets, n_head, n_seq, ways):
    length = grads.shape[1]
    width = qkv_weight_t.shape[1]
    tsd = length // n_seq
    groups = n_seq // 8
    rows = tsd // 2
    lines, _, piece, _ = weights.shape
    vmem = pl.BlockSpec(memory_space=pltpu.VMEM)
    out, weights, small = pl.pallas_call(
        functools.partial(finish_kernel, n_head, n_seq, ways, groups, buckets),
        out_shape=[
            jax.ShapeDtypeStruct((groups, 2, rows, width), BF16),
            jax.ShapeDtypeStruct(weights.shape, BF16),
            jax.ShapeDtypeStruct((n_head, lines, 2, 8, 128), F32),
        ],
        in_specs=[vmem] * 6,
        out_specs=[vmem] * 3,
        scratch_shapes=[
            pltpu.VMEM((n_head, lines, 2, 8, 128), F32),
            pltpu.VMEM((groups, 4, tsd, width), BF16),
            pltpu.VMEM((groups, 4, tsd, width), F32),
            pltpu.VMEM((groups, 4, tsd, width), BF16),
            pltpu.VMEM((groups, 4, rows, width), BF16),
            pltpu.VMEM((groups, 2, rows, width), BF16),
            pltpu.VMEM((groups, 4, 2, rows, width), BF16),
            pltpu.VMEM((groups, 4, rows, width), BF16),
            pltpu.VMEM((lines, piece, width), BF16),
            pltpu.VMEM((lines, piece, width), BF16),
            pltpu.VMEM((lines, piece, width), BF16),
            pltpu.VMEM((piece, width), BF16),
            pltpu.VMEM((2 * n_head, lines, 8, 128), F32),
            pltpu.VMEM((lines, 8, 128), F32),
            pltpu.VMEM((lines, 8, 128), F32),
            pltpu.VMEM((8, 128), F32),
            pltpu.VMEM((lines, 8, 128), F32),
            pltpu.SemaphoreType.DMA((3, groups, 4)),
            pltpu.SemaphoreType.DMA((3, groups, 4)),
            pltpu.SemaphoreType.DMA((1 + lines,)),
            pltpu.SemaphoreType.DMA((1 + lines,)),
            pltpu.SemaphoreType.DMA((2, lines)),
            pltpu.SemaphoreType.DMA((2, lines)),
            pltpu.SemaphoreType.DMA((2, 2 * n_head)),
            pltpu.SemaphoreType.DMA((2, 2 * n_head)),
            pltpu.SemaphoreType.DMA((2, lines)),
            pltpu.SemaphoreType.DMA((2, lines)),
        ],
        compiler_params=pltpu.CompilerParams(
            collective_id=6, has_side_effects=True, vmem_limit_bytes=56 * MB
        ),
        name="finish_sums",
    )(grads, qkv_weight_t, weights, small.reshape(n_head, lines, 2, 8, 128), gains, tables)
    return out.reshape(groups, tsd, width), weights, small.reshape(n_head * n_seq, 8, 128)


def send_home(blocks, own, seqs, n_head, n_seq):
    groups = blocks.shape[0]
    assert groups == own
    head, seq = lax.axis_index("head"), lax.axis_index("seq")
    inner = line_to_batch(seq // 2, seqs) % own
    rounds = []
    for k in range(own):
        pairs = []
        for a in range(n_head):
            for q in range(n_seq):
                line, y, x, core = q // 2, q % 2, a // 2, a % 2
                batch = line_to_batch(line, seqs)
                v = (k + batch % own) % groups
                home = core * 4 * groups + v * 4 + (x ^ (line // 2 % 2)) * 2 + y
                pairs.append((a * n_seq + q, batch // own * n_seq + home))
        piece = lax.dynamic_index_in_dim(blocks, (k + inner) % groups, 0, keepdims=False) if own > 1 else blocks[0]
        rounds.append(lax.ppermute(piece, ("head", "seq"), pairs))
    if own == 1:
        return rounds[0][None]
    rounds = jnp.stack(rounds)
    at = seq // 4 % groups
    return jnp.stack([lax.dynamic_index_in_dim(rounds, (at - i) % own, 0, keepdims=False) for i in range(own)])


def outputs_kernel(
    columns, n_seq, first_ref, last_ref, small, gain, qkv_ref, proj_ref, router_ref, ffn_ref, attn_ref, bias_ref, table_ref
):
    heads = first_ref.shape[0] + 1
    share = proj_ref.shape[0] // heads
    for n in range(heads):
        rows = last_ref[...] if n == heads - 1 else first_ref[n]
        qkv_ref[n * columns : (n + 1) * columns] = rows[:columns].astype(F32)
        proj_ref[n * share : (n + 1) * share] = rows[columns : columns + share].astype(F32)
    chunks = gain.shape[0]
    extra = 8 - chunks
    for n in range(chunks):
        router_ref[:, n * 128 : (n + 1) * 128] = small[:, n, :]
        ffn_ref[n : n + 1, :] = small[n // extra, chunks + n % extra : chunks + n % extra + 1, :]
        at = chunks + n
        row = small[at // extra, chunks + at % extra : chunks + at % extra + 1, :]
        attn_ref[n : n + 1, :] = row / gain[n : n + 1, :]
    at = 2 * chunks // extra
    bias_ref[...] = small[at, chunks : chunks + 1, :]
    table_ref[...] = small[8 + lax.axis_index("head"), chunks : chunks + 1, :]


def outputs(first, last, small, gain, columns, hidden, n_seq):
    heads, width = first.shape[0] + 1, first.shape[-1]
    assert 2 * (width // 128) % (8 - width // 128) == 0
    vmem = pl.BlockSpec(memory_space=pltpu.VMEM)
    return pl.pallas_call(
        functools.partial(outputs_kernel, columns, n_seq),
        out_shape=[
            jax.ShapeDtypeStruct((heads * columns, width), F32),
            jax.ShapeDtypeStruct((hidden, width), F32),
            jax.ShapeDtypeStruct((small.shape[0], width), F32),
            jax.ShapeDtypeStruct(gain.shape, F32),
            jax.ShapeDtypeStruct(gain.shape, F32),
            jax.ShapeDtypeStruct((1, 128), F32),
            jax.ShapeDtypeStruct((1, 128), F32),
        ],
        in_specs=[vmem] * 4,
        out_specs=[vmem] * 7,
        compiler_params=pltpu.CompilerParams(vmem_limit_bytes=32 * MB),
        name="outputs",
    )(first.reshape(heads - 1, -1, width), last.reshape(-1, width), small, gain)


def last_kernel(sum_ref, x_ref, mid_ref, gain, out_ref):
    gains = jnp.concatenate([gain[n : n + 1, :] for n in range(gain.shape[0])], axis=1)
    x = x_ref[...]
    inverse = rms_inverse(x)
    unit = x * inverse
    scaled = sum_ref[...].astype(F32) * gains
    inner = jnp.mean(scaled * unit, axis=-1, keepdims=True)
    out_ref[...] = (mid_ref[...] + inverse * (scaled - unit * inner)).astype(BF16)


def last_step(sums, x, mid, gain):
    rows, width = x.shape
    block = pl.BlockSpec((rows // 4, width), lambda t: (t, 0))
    return pl.pallas_call(
        last_kernel,
        grid=(4,),
        out_shape=jax.ShapeDtypeStruct((rows, width), BF16),
        in_specs=[block, block, block, pl.BlockSpec(gain.shape, lambda t: (0, 0))],
        out_specs=block,
        compiler_params=pltpu.CompilerParams(vmem_limit_bytes=32 * MB),
        name="last_step",
    )(sums, x, mid, gain)


def rms_inverse(values):
    return lax.rsqrt(jnp.mean(values * values, axis=-1, keepdims=True) + eps)


def dot(a, b, dims, precision=None):
    return lax.dot_general(a, b, (dims, ((), ())), preferred_element_type=F32, precision=precision)


def local(
    n_head,
    n_seq,
    tokens,
    attn_gain,
    qkv_weight,
    bias_table,
    proj_weight,
    ffn_gain,
    router_weight,
    router_bias,
    expert_in,
    expert_out,
    bucket,
    expert_choice,
    priority,
    out_grad,
):
    tsd, seqs, width = tokens.shape
    buckets, heads_here = bias_table.shape
    head_dim = qkv_weight.shape[1] // (3 * heads_here)
    hidden = heads_here * head_dim
    length = bucket.shape[0] // 2
    own = out_grad.shape[1]
    ways = n_seq // seqs
    qlen = length // ways
    experts = router_weight.shape[1]
    devices = n_head * n_seq
    assert ways == 2 and n_head == 4 and own * n_head == seqs and experts == devices
    seq_index = lax.axis_index("seq")
    head_index = lax.axis_index("head")
    half = seq_index % ways

    qkv_weight_t = qkv_weight.T
    offsets = bucket[None, :]
    normed1, qkv_t, strips_f, strips_b = gather_rows(
        tokens, attn_gain.reshape(width // 128, 128), qkv_weight_t, offsets, bias_table.T, n_head, n_seq, ways
    )
    qkv_t = qkv_t.reshape(heads_here, 3, head_dim, length)

    half_at = half.reshape(1)
    attended_t, lse = attend_forward(half_at, strips_f, qkv_t, qlen, tsd)

    spread, proj_full = to_residual(
        attended_t.reshape(hidden, qlen), proj_weight, own, ways, seqs, n_head, tsd
    )
    proj_full = proj_full.reshape(n_head * hidden, width)
    att_all = spread.reshape(own, n_head * hidden, tsd)
    branch = jnp.einsum("bcp,cd->bpd", att_all, proj_full, preferred_element_type=F32)
    rows = own * tsd
    x_own = lax.dynamic_slice_in_dim(tokens, head_index * own, own, 1).astype(F32)
    x_own = jnp.moveaxis(x_own, 1, 0).reshape(rows, width)
    mid = x_own + branch.reshape(rows, width)
    inv2 = rms_inverse(mid)
    normed2 = (mid * inv2 * ffn_gain).astype(BF16)
    logits = dot(normed2, router_weight, ((1,), (0,))) + router_bias
    gates = jax.nn.softmax(logits, axis=1)
    route = expert_choice.T.reshape(rows)
    order = priority.T.reshape(rows)
    same = (route[:, None] == route[None, :]) & (order[None, :] < order[:, None])
    rank = jnp.sum(same.astype(jnp.int32), axis=1)
    capacity = max(2, (5 * rows + 4 * experts - 1) // (4 * experts))
    mains = capacity // 16
    tails = -(-(capacity - 16 * mains) // 4)
    keep = rank < capacity
    chosen = (route[:, None] == jnp.arange(experts, dtype=jnp.int32)[None, :]).astype(F32)
    gate = jnp.sum(gates * chosen, axis=1)
    upstream = jnp.moveaxis(out_grad, 1, 0).astype(F32).reshape(rows, width)
    grad_rows = (gate[:, None] * upstream).astype(BF16)
    beside = jnp.concatenate([normed2, grad_rows], axis=1)
    below = jnp.concatenate([normed2, grad_rows], axis=0)
    fold = width // 2
    placing_mains, placing_tails, sending = [], [], []
    for j in range(mains):
        at = jnp.where(keep & (rank // 16 == j), route * 16 + rank % 16, -1)
        placing = (at[None, :] == jnp.arange(experts * 16, dtype=jnp.int32)[:, None]).astype(BF16)
        placing_mains.append(placing)
        sending.append(dot(placing, beside, ((1,), (0,))).astype(BF16).reshape(experts, 16, 2 * width))
    for u in range(tails):
        from_rank = rank - 16 * mains - 4 * u
        at = jnp.where(keep & (from_rank >= 0) & (from_rank < 4), route * 16 + from_rank, -1)
        at = jnp.concatenate([at, jnp.where(at >= 0, at + 4, -1)])
        lines = jnp.arange(experts * 16, dtype=jnp.int32)[:, None]
        left, right = (at[None, :] == lines).astype(BF16), (at[None, :] + 8 * (at[None, :] >= 0) == lines).astype(BF16)
        placing_tails.append((left, right))
        tail = dot(left, below[:, :fold], ((1,), (0,))) + dot(right, below[:, fold:], ((1,), (0,)))
        sending.append(tail.astype(BF16).reshape(experts, 16, fold))
    back, *kept = run_experts(
        jnp.concatenate(sending, axis=2), expert_in[0], expert_out[0], n_head, n_seq, mains, tails
    )
    grad_expert_in, grad_expert_out = expert_weights(*kept)
    grad_expert_in, grad_expert_out = grad_expert_in[None], grad_expert_out[None]
    expert_rows, grad_disp = 0.0, 0.0
    for j, placing in enumerate(placing_mains):
        main = back[:, :, j * 2 * width : (j + 1) * 2 * width].reshape(experts * 16, 2 * width)
        main = dot(placing, main, ((0,), (0,)))
        expert_rows, grad_disp = expert_rows + main[:, :width], grad_disp + main[:, width:]
    for u, halves in enumerate(placing_tails):
        at = mains * 2 * width + u * fold
        tail = back[:, :, at : at + fold].reshape(experts * 16, fold)
        tail = jnp.concatenate([dot(placing, tail, ((0,), (0,))) for placing in halves], axis=1)
        expert_rows, grad_disp = expert_rows + tail[:rows], grad_disp + tail[rows:]

    output = mid + gate[:, None] * expert_rows
    output = jnp.moveaxis(output.astype(BF16).reshape(own, tsd, width), 0, 1)
    grad_gate = jnp.sum(upstream * expert_rows, axis=1)
    grad_logits = gates * (chosen - gate[:, None]) * grad_gate[:, None]
    grad_router_bias = jnp.sum(grad_logits, axis=0)
    grad_normed2 = grad_disp + dot(grad_logits, router_weight.astype(F32), ((1,), (1,)), HIGH)
    scaled2 = grad_normed2 * ffn_gain
    unit2 = mid * inv2
    grad_ffn_gain = jnp.sum(grad_normed2 * unit2, axis=0)
    grad_mid = upstream + inv2 * (scaled2 - unit2 * jnp.mean(scaled2 * unit2, axis=-1, keepdims=True))
    grad_branch = grad_mid.astype(BF16).reshape(own, tsd, width)

    grad_qkv_t, grad_table, gain_parts, weights_first, weights_last = attend_backward(
        offsets, strips_b, qkv_t, attended_t, lse, qkv_weight_t, att_all, grad_branch, proj_full, normed1, buckets,
        n_head, n_seq,
    )
    grad_qkv_t = grad_qkv_t.reshape(3 * hidden, length)

    late_logits, late_rows, gain_parts = lax.optimization_barrier((grad_logits, normed2, gain_parts))
    grad_router_t = dot(late_logits, late_rows.astype(F32), ((0,), (0,)), HIGH)
    extras = jnp.concatenate([grad_ffn_gain, jnp.zeros((width,), F32), grad_router_bias])
    assert devices >= 8 + n_head and buckets * heads_here <= 128 and 2 * width + experts <= 8 * 256
    lanes = 128
    chunks = width // lanes
    extras = jnp.pad(extras, (0, devices * (8 - chunks) * lanes - extras.shape[0]))
    small = jnp.concatenate(
        [grad_router_t.reshape(experts, chunks, lanes), extras.reshape(devices, 8 - chunks, lanes)], axis=1
    )
    grad_normed1_own, weights_last, small = finish_sums(
        grad_qkv_t, qkv_weight_t, weights_last, small, gain_parts, grad_table, buckets, n_head, n_seq, ways
    )
    grad_normed1_own = send_home(grad_normed1_own, own, seqs, n_head, n_seq)
    grad_qkv_weight, grad_proj_weight, grad_router, grad_ffn_gain, grad_attn_gain, grad_bias, grad_table = outputs(
        weights_first, weights_last, small, attn_gain.reshape(chunks, lanes), 3 * head_dim, hidden, n_seq
    )
    grad_qkv_weight = grad_qkv_weight.T
    grad_router_weight = grad_router.T
    grad_ffn_gain, grad_attn_gain = grad_ffn_gain.reshape(width), grad_attn_gain.reshape(width)
    grad_router_bias = grad_bias[0, :experts]
    grad_bias_table = grad_table[0, : heads_here * buckets].reshape(heads_here, buckets).T
    grad_tokens = last_step(
        grad_normed1_own.reshape(rows, width), x_own, grad_mid, attn_gain.reshape(chunks, lanes)
    )
    grad_tokens = jnp.moveaxis(grad_tokens.reshape(own, tsd, width), 0, 1)
    return (
        output,
        grad_tokens,
        grad_attn_gain,
        grad_qkv_weight,
        grad_bias_table,
        grad_proj_weight,
        grad_ffn_gain,
        grad_router_weight,
        grad_router_bias,
        grad_expert_in,
        grad_expert_out,
    )


def solution(mesh):
    placed = (
        P("seq", None, None),
        P(),
        P(None, "head"),
        P(None, "head"),
        P("head", None),
        P(),
        P(),
        P(),
        P(("head", "seq"), None, None),
        P(("head", "seq"), None, None),
        P(),
        P("seq", "head"),
        P("seq", "head"),
        P("seq", "head", None),
    )
    return jax.shard_map(
        functools.partial(local, mesh.shape["head"], mesh.shape["seq"]),
        mesh=mesh,
        in_specs=placed,
        out_specs=(
            P("seq", "head", None),
            P("seq", "head", None),
            P(),
            P(None, "head"),
            P(None, "head"),
            P("head", None),
            P(),
            P(),
            P(),
            P(("head", "seq"), None, None),
            P(("head", "seq"), None, None),
        ),
        check_vma=False,
    )
```

time: 2670 us -> 390 us (0.15); the launches traced: 2630 us -> 383 us
  local copies, waits for them, and re-layouts: 1460 us -> 9.79 us
  matrix products: 445 us -> 9.6 us
  Pallas kernels: 0 us -> 349 us
  waiting for transfers between devices: 329 us -> 0.01 us
  other arithmetic: 295 us -> 7.84 us
  blocking collectives: 60.8 us -> 0 us
    unnamed x110 -> x32, local copies, waits for them, and re-layouts: 1210 us -> 3.84 us
    dot_general x43 -> x10, matrix products: 445 us -> 9.6 us  [the longest x9 7.18 us: dot(): lax.dot_general(a, b, (dims, ((), ())), preferred_element_type=F32, preci...]
    pallas_call x0 -> x9, Pallas kernels: none -> 349 us  [the longest x1 97.9 us: attend_backward(): pl.pallas_call(functools.partial(backward_kernel, length, qlen, hd, tsd,...]
    reduce_scatter x3 -> x0, waiting for transfers between devices: 250 us -> none  [the longest x1 197 us: local(): lax.psum_scatter(jnp.concatenate([grad_k.reshape(count, seqs, hidden_widt...]
    dynamic_update_slice x13 -> x0, other arithmetic: 158 us -> none  [the longest x12 158 us: local(): lax.map(attend_block, (group_query, group_keys, group_vals))]
    reduce_sum x9 -> x1, other arithmetic: 105 us -> 1.33 us  [local(): grad_gate = jnp.sum(upstream * expert_rows, axis=1)]
    reshape x14 -> x0, local copies, waits for them, and re-layouts: 87.1 us -> none  [the longest x1 38.6 us: toeplitz(): tiled[:, :rows * (count - 1)].reshape(heads, rows, count - 1)[:, :, :cols]]
    psum x2 -> x0, blocking collectives: 60.8 us -> none  [the longest x1 43.5 us: local(): lax.psum((grad_attn_gain, grad_ffn_gain, grad_router_weight, grad_router_...]
  transfers between devices with their start and end apart: 12 -> 1, of which waited for: 7 -> 0; matrix products, arithmetic and copies ran while one was open for 56% -> 0% of each run, Pallas kernels for 0% -> 4%
where the time goes in v2:
time: 390 us; the launch traced here: 383 us
  Pallas kernels  349 us (89%)
  local copies, waits for them, and re-layouts  9.79 us (3%)
  matrix products  9.6 us (2%)
  other arithmetic  7.84 us (2%)
  starting transfers between devices  4.97 us (1%)
    pallas_call x1, Pallas kernels, attend_backward(): pl.pallas_call(functools.partial(backward_kernel, length, qlen, hd, tsd,...  97.9 us
    pallas_call x1, Pallas kernels, run_experts(): pl.pallas_call(functools.partial(experts_kernel, n_head, n_seq, mains, ta...  93.1 us
    pallas_call x1, Pallas kernels, finish_sums(): pl.pallas_call(functools.partial(finish_kernel, n_head, n_seq, ways, grou...  48.5 us
    pallas_call x1, Pallas kernels, gather_rows(): pl.pallas_call(functools.partial(gather_kernel, n_seq, ways, seqs, tsd, s...  45.6 us
    pallas_call x1, Pallas kernels, attend_forward(): pl.pallas_call(functools.partial(forward_kernel, length, qlen, hd, tsd, b...  27.3 us
    pallas_call x1, Pallas kernels, to_residual(): pl.pallas_call(functools.partial(to_residual_kernel, own, ways, seqs, n_h...  20.1 us
    pallas_call x1, Pallas kernels, expert_weights(): pl.pallas_call(weights_kernel, grid=(hidden // tile,), out_shape=[jax.Sha...  12.9 us
  transfers between devices with their start and end apart: 1, of which 0 were waited for; matrix products, arithmetic and copies ran while one was open for 0% of the time, Pallas kernels for 4%

profile of v2, /device:TPU:12, one launch (start us, length us, event | category | flops | bytes accessed | tf_op | source)
XLA Modules:
  0.0 382.6 jit_solution(17519041242926031915)
XLA Ops:
  0.7 1.1 convert_reduce_fusion
  1.8 0.7 add_select_fusion.2
  2.5 3.5 constant_dynamic-slice_fusion
  6.0 45.6 %gather_rows.1 = (bf16[4096,768]{1,0:T(8,128)(2,1)}, bf16[576,4096]{1,0:T(8,128)(2,1)}, f32[3,8064,128]{2,1,0:T(8,128)}, f32[3,8064,128]{2,1,0:T(8,128)}) custom-call(bf16[512,4,768]{2,1,0:T(4,128)(2,1)} %tokens.1, f32[6,128]{1,0:T(8,128)} %bitcast.65, bf16[576,768]{1,0:T(8,128)(2,1)} %bitcast.74, s32[1,8192]{1,0:T(1,128)} %bitcast.91, f32[3,32]{1,0:T(4,128)} %bitcast.99), custom_call_target="tpu_custom_call" | custom-call | tf_op jit(solution)/shard_map/gather_rows/pallas_call | solution.py:782
  51.7 27.3 %attend_forward.1 = (bf16[3,64,2048]{2,1,0:T(8,128)(2,1)}, f32[3,1,2048]{2,1,0:T(1,128)}) custom-call(s32[1]{0:T(128)} %bitcast.1.half_ref, f32[3,8064,128]{2,1,0:T(8,128)} %get-tuple-element.44.strip_ref, bf16[3,3,64,4096]{3,2,1,0:T(8,128)(2,1)} %bitcast.68, bf16[3,3,64,4096]{3,2,1,0:T(8,128)(2,1)} %bitcast.69, bf16[3,3,64,4096]{3,2,1,0:T(8,128)(2,1)} %bitcast.70), custom_call_target="tpu_custom_call" | custom-call | flops 6442450944 | bytes 7864320 | tf_op jit(solution)/shard_map/attend_forward/pallas_call | solution.py:151
  79.0 20.1 %to_residual.1 = (bf16[1,4,192,512]{3,2,1,0:T(8,128)(2,1)}, bf16[4,192,768]{2,1,0:T(8,128)(2,1)}) custom-call(bf16[192,2048]{1,0:T(8,128)(2,1)} %bitcast.81, bf16[192,768]{1,0:T(8,128)(2,1)} %proj.1), custom_call_target="tpu_custom_call" | custom-call | tf_op jit(solution)/shard_map/to_residual/pallas_call | solution.py:882
  99.1 2.4 multiply_reduce_fusion.2
  102.9 0.7 fusion.1
  103.6 1.0 convolution_convert_fusion
  104.6 0.7 fusion.14
  105.3 1.4 pad_maximum_fusion.sending
  106.8 93.1 %run_experts.1 = (bf16[32,16,1920]{2,1,0:T(8,128)(2,1)}, bf16[768,768]{1,0:T(8,128)(2,1)}, bf16[768,768]{1,0:T(8,128)(2,1)}, bf16[768,3072]{1,0:T(8,128)(2,1)}, bf16[768,3072]{1,0:T(8,128)(2,1)}) custom-call(bf16[32,16,1920]{2,1,0:T(8,128)(2,1)} %pad_maximum_fusion.sending, bf16[768,3072]{1,0:T(8,128)(2,1)} %bitcast.79, bf16[3072,768]{1,0:T(8,128)(2,1)} %bitcast.80), custom_call_target="tpu_custom_call" | custom-call | tf_op jit(solution)/shard_map/run_experts/pallas_call | solution.py:1054
  199.9 1.0 slice.34
  200.9 0.8 fusion
  201.7 0.8 fusion.2
  202.5 0.8 copy-done.12
  203.4 1.0 fusion.19
  204.5 1.3 fusion.5
  206.0 1.4 multiply_reduce_fusion
  207.3 1.9 convert_bitcast_fusion
  209.2 97.9 %attend_backward.1 = (bf16[3,192,4096]{2,1,0:T(8,128)(2,1)}, f32[3,8,128]{2,1,0:T(8,128)}, f32[3,8,768]{2,1,0:T(8,128)}, bf16[2,4,2,32,768]{4,3,2,1,0:T(8,128)(2,1)}, bf16[4,2,32,768]{3,2,1,0:T(8,128)(2,1)}) custom-call(s32[1,8192]{1,0:T(1,128)} %bitcast.92, f32[3,8064,128]{2,1,0:T(8,128)} %get-tuple-element.50.strip_ref, bf16[3,3,64,4096]{3,2,1,0:T(8,128)(2,1)} %bitcast.71, ...), custom_call_target="tpu_custom_call" | custom-call | tf_op jit(solution)/shard_map/attend_backward/pallas_call | solution.py:475
  307.2 0.5 fusion.38
  307.7 0.7 pad_maximum_fusion.4.small_ref
  308.4 48.5 %finish_sums.1 = (bf16[1,2,256,768]{3,2,1,0:T(8,128)(2,1)}, bf16[4,2,32,768]{3,2,1,0:T(8,128)(2,1)}, f32[4,4,2,8,128]{4,3,2,1,0:T(8,128)}) custom-call(bf16[576,4096]{1,0:T(8,128)(2,1)} %bitcast.78, bf16[576,768]{1,0:T(8,128)(2,1)} %bitcast.76, bf16[4,2,32,768]{3,2,1,0:T(8,128)(2,1)} %get-tuple-element.54.weights, ...), custom_call_target="tpu_custom_call" | custom-call | tf_op jit(solution)/shard_map/finish_sums/pallas_call | solution.py:1264
  356.9 5.0 %collective-permute-start = (bf16[512,768]{1,0:T(8,128)(2,1)}, bf16[512,768]{1,0:T(8,128)(2,1)S(1)}, u32[]{:S(2)}, u32[]{:S(2)}) collective-permute-start(bf16[512,768]{1,0:T(8,128)(2,1)} %bitcast.102), channel_id=1, source_target_pairs={{0,0},{1,1},{2,16},{3,17},{4,10},{5,11},{6,26},{7,27},{8,4},{9,5},... | collective-permute-start | bytes 2359304 | tf_op jit(solution)/shard_map/ppermute | solution.py:1326
  362.0 1.6 outputs.1
  363.6 0.5 slice_bitcast_fusion
  364.1 0.7 reshape_squeeze.3
  364.8 1.3 copy-done.7
  366.1 1.3 copy-done.8
  367.4 12.9 %expert_weights.1 = (f32[768,3072]{1,0:T(8,128)}, f32[3072,768]{1,0:T(8,128)}) custom-call(bf16[768,768]{1,0:T(8,128)(2,1)S(1)} %copy-done.7, bf16[768,768]{1,0:T(8,128)(2,1)S(1)} %copy-done.8, bf16[768,3072]{1,0:T(8,128)(2,1)} %get-tuple-element.73.act_ref, bf16[768,3072]{1,0:T(8,128)(2,1)} %get-tuple-element.74.pre_ref), custom_call_target="tpu_custom_call" | custom-call | flops 7247757312 | bytes 28311552 | tf_op jit(solution)/shard_map/expert_weights/pallas_call | solution.py:1099
  380.2 2.1 last_step.1
  (45 shorter events, 1.8 us)
Async XLA Ops:
  0.6 101.1 %copy-start = (bf16[768,32]{0,1:T(8,128)(2,1)S(1)}, bf16[768,32]{0,1:T(8,128)(2,1)}, u32[]{:S(2)}) copy-start(bf16[768,32]{0,1:T(8,128)(2,1)} %param.20) | copy-start | bytes 147460
  6.0 93.1 %copy-start.10 = (bf16[512,1,768]{2,1,0:T(2,128)(2,1)}, bf16[512,1,768]{2,1,0:T(2,128)(2,1)S(1)}, u32[]{:S(2)}) copy-start(bf16[512,1,768]{2,1,0:T(2,128)(2,1)S(1)} %constant_dynamic-slice_fusion) | copy-start | bytes 2359300
  99.1 2.5 copy-start.14
  101.5 0.7 copy-start.15
  101.6 1.0 copy-start.13
  101.6 1.1 copy-start.9
  201.7 1.5 copy-start.12
  308.4 53.5 %copy-start.11 = (bf16[512,1,768]{2,1,0:T(2,128)(2,1)S(1)}, bf16[512,1,768]{2,1,0:T(2,128)(2,1)}, u32[]{:S(2)}) copy-start(bf16[512,1,768]{2,1,0:T(2,128)(2,1)} %copy-done.10) | copy-start | bytes 2359300
  356.9 5.1 %copy-start.3 = (bf16[2,4,2,32,768]{4,3,2,1,0:T(8,128)(2,1)S(1)}, bf16[2,4,2,32,768]{4,3,2,1,0:T(8,128)(2,1)}, u32[]{:S(2)}) copy-start(bf16[2,4,2,32,768]{4,3,2,1,0:T(8,128)(2,1)} %get-tuple-element.61) | copy-start | bytes 2359300
  356.9 5.1 %copy-start.4 = (bf16[4,2,32,768]{3,2,1,0:T(8,128)(2,1)S(1)}, bf16[4,2,32,768]{3,2,1,0:T(8,128)(2,1)}, u32[]{:S(2)}) copy-start(bf16[4,2,32,768]{3,2,1,0:T(8,128)(2,1)} %get-tuple-element.62) | copy-start | bytes 1179652
  356.9 5.1 %copy-start.5 = (f32[4,4,2,8,128]{4,3,2,1,0:T(8,128)S(1)}, f32[4,4,2,8,128]{4,3,2,1,0:T(8,128)}, u32[]{:S(2)}) copy-start(f32[4,4,2,8,128]{4,3,2,1,0:T(8,128)} %get-tuple-element.63) | copy-start | bytes 393220
  356.9 5.1 %copy-start.6 = (f32[768]{0:T(1024)S(1)}, f32[768]{0:T(1024)}, u32[]{:S(2)}) copy-start(f32[768]{0:T(1024)} %param.15) | copy-start | bytes 9220
  356.9 23.3 %collective-permute-start = (bf16[512,768]{1,0:T(8,128)(2,1)}, bf16[512,768]{1,0:T(8,128)(2,1)S(1)}, u32[]{:S(2)}, u32[]{:S(2)}) collective-permute-start(bf16[512,768]{1,0:T(8,128)(2,1)} %bitcast.102), channel_id=1, source_target_pairs={{0,0},{1,1},{2,16},{3,17},{4,10},{5,11},{6,26},{7,27},{8,4},{9,5},... | collective-permute-start | bytes 2359304 | tf_op jit(solution)/shard_map/ppermute | solution.py:1326
  364.8 1.3 copy-start.7
  366.1 1.3 copy-start.8
  367.3 12.9 %copy-start.2 = (f32[512,768]{1,0:T(8,128)S(1)}, f32[512,768]{1,0:T(8,128)}, u32[]{:S(2)}) copy-start(f32[512,768]{1,0:T(8,128)} %get-tuple-element.82.mid_ref) | copy-start | bytes 4718596
  380.2 2.1 copy-start.1
